TPU v7x, 32 devices: a whole 2x2x4 slice. The times are simulated.
32 devices in a mesh: pipe: 4 (over x, core), seq: 2 (over y), mp: 4 (over z).
Axes of the slice: x: 2, y: 2, z: 4, core: 2. Of those that a mesh axis runs over, the one named last changes fastest.
Arguments:
- enc_in: bfloat16 [2, 128, 4096], P(None, 'seq'), may hold values from -6 to 6
- dec_in: bfloat16 [2, 128, 4096], P(None, 'seq'), may hold values from -6 to 6
- doc_ids: int32 [2, 128], replicated, may hold values from 0 to 1, as said below
- enc_sections: int32 [1], replicated, may hold values from 1 to 3
- norm_gain: float32 [4, 4096], P('pipe'), may hold values from 0.1 to 1.9
- q_weight: bfloat16 [4, 4096, 2048], P('pipe', None, 'mp'), may hold values from -0.09375 to 0.09375
- k_weight: bfloat16 [4, 4096, 2048], P('pipe', None, 'mp'), may hold values from -0.09375 to 0.09375
- v_weight: bfloat16 [4, 4096, 2048], P('pipe', None, 'mp'), may hold values from -0.09375 to 0.09375
- o_weight: bfloat16 [4, 2048, 4096], P('pipe', 'mp'), may hold values from -1.25 to 1.25
- out_grad: bfloat16 [2, 128, 4096], P(None, 'seq'), may hold values from -6 to 6
Outputs:
- section_out: bfloat16 [4, 2, 128, 4096], P('pipe', None, 'seq', 'mp')
- section_grad: bfloat16 [4, 2, 2, 128, 4096], P('pipe', None, None, 'seq', 'mp')
Inputs may be any that keep to these rules, and one draw needn't show every extreme that they name: `doc_ids`: ids of the two documents that each micro-batch's window holds, shared by its encoder and decoder positions; 0 up to a boundary, 1 after it, each document 64 // 2 or more positions long. Sections with an index below enc_sections[0] are encoder sections, the others decoder sections.
All inputs are finite; a program needn't handle non-finite values.
Results may differ from a plain program's by a relative error of at most 0.034.
Values may be sent and summed in bfloat16 or wider, within the bound.
A program may use at most 192 MiB of HBM per device.

v0:
```python
import jax
import jax.numpy as jnp
from jax import lax
from jax.sharding import PartitionSpec as P

HEADS = 8
HS = 256


epsilon = 1e-06


def shifted(x, axis, by):
    length = lax.axis_size(axis)
    pairs = [(i, i + by) for i in range(length) if 0 <= i + by < length]
    return lax.ppermute(x, axis, pairs)


def row_norm(stream, stream_gain):
    values = stream.astype(jnp.float32)
    factor = lax.rsqrt(jnp.mean(values * values, axis=-1, keepdims=True) + epsilon)
    return ((values * factor * stream_gain).astype(jnp.bfloat16), factor)


def head_norm(projected, head_count):
    shaped = projected.reshape(projected.shape[0], head_count, -1)
    factor = lax.rsqrt(jnp.mean(shaped * shaped, axis=-1, keepdims=True) + epsilon)
    return ((shaped * factor).astype(jnp.bfloat16), factor)


def norm_back(stream, factor, stream_gain, incoming):
    values = stream.astype(jnp.float32)
    scaled = stream_gain * incoming
    return factor * (
        scaled - values * factor * factor * jnp.mean(scaled * values, axis=-1, keepdims=True)
    )


def head_back(normed, factor, incoming):
    values = normed.astype(jnp.float32)
    return factor * (incoming - values * jnp.mean(incoming * values, axis=-1, keepdims=True))


def attend_keys(queries, key_all, same_doc, score_scale):
    scores = (
        jnp.einsum("thd,khd->htk", queries, key_all, preferred_element_type=jnp.float32)
        * score_scale
    )
    weights = jnp.where(same_doc[None], jnp.exp(scores), 0.0)
    return (weights, jnp.sum(weights, axis=-1))


def head_total(values):
    return lax.psum(values.astype(jnp.bfloat16), "mp").astype(jnp.float32)


def per_device(
    enc_in,
    dec_in,
    doc_ids,
    enc_sections,
    norm_gain,
    q_weight,
    k_weight,
    v_weight,
    o_weight,
    out_grad,
):
    section_count = lax.axis_size("pipe")
    section_id = lax.axis_index("pipe")
    mp_count = lax.axis_size("mp")
    mp_index = lax.axis_index("mp")
    seq_index = lax.axis_index("seq")
    batch_count, tok_rows, model_width = enc_in.shape
    share_width = model_width // mp_count
    local_heads = HEADS // mp_count
    score_scale = HS ** (-0.5)
    tick_count = batch_count + section_count - 1
    encoder = section_id < enc_sections[0]
    stream_gain = norm_gain[0]
    query_map = q_weight[0]
    key_map = k_weight[0]
    value_map = v_weight[0]
    out_map = o_weight[0]

    def cut_share(stream):
        return lax.dynamic_slice_in_dim(
            stream, mp_index * share_width, share_width, stream.ndim - 1
        )

    out_slots = [jnp.zeros((tok_rows, share_width), jnp.bfloat16) for slot_id in range(batch_count)]
    stored = []
    for tick_id in range(tick_count):
        batch_id = tick_id - section_id
        if tick_id > 0:
            recv_enc, recv_dec = shifted((send_enc, send_dec), "pipe", 1)
        if tick_id < batch_count:
            start_enc = enc_in[tick_id]
            start_dec = dec_in[tick_id]
            if tick_id == 0:
                recv_enc = jnp.zeros_like(start_enc)
                recv_dec = jnp.zeros_like(start_dec)
            recv_enc = jnp.where(section_id == 0, start_enc, recv_enc)
            recv_dec = jnp.where(section_id == 0, start_dec, recv_dec)
        enc_full, dec_full = (recv_enc, recv_dec)
        source = jnp.where(encoder, enc_full, dec_full)
        q_in, q_factor = row_norm(source, stream_gain)
        m_in, m_factor = row_norm(enc_full, stream_gain)
        queries, q_head = head_norm(
            jnp.dot(q_in, query_map, preferred_element_type=jnp.float32), local_heads
        )
        key_rows, k_head = head_norm(
            jnp.dot(m_in, key_map, preferred_element_type=jnp.float32), local_heads
        )
        value_rows = jnp.dot(m_in, value_map, preferred_element_type=jnp.float32).astype(
            jnp.bfloat16
        )
        value_rows = value_rows.reshape(tok_rows, local_heads, HS)
        key_all, value_all = (
            lax.all_gather(key_rows, "seq", axis=0, tiled=True),
            lax.all_gather(value_rows, "seq", axis=0, tiled=True),
        )
        doc_row = lax.dynamic_index_in_dim(
            doc_ids, jnp.clip(batch_id, 0, batch_count - 1), 0, keepdims=False
        )
        doc_query = lax.dynamic_slice_in_dim(doc_row, seq_index * tok_rows, tok_rows)
        same_doc = doc_query[:, None] == doc_row[None, :]
        weights, totals = attend_keys(queries, key_all, same_doc, score_scale)
        summed = jnp.einsum(
            "htk,khd->thd",
            weights.astype(jnp.bfloat16),
            value_all,
            preferred_element_type=jnp.float32,
        )
        attended = (summed / jnp.transpose(totals)[:, :, None]).astype(jnp.bfloat16)
        partial_out = jnp.dot(
            attended.reshape(tok_rows, -1), out_map, preferred_element_type=jnp.float32
        )
        branch = head_total(partial_out[None])[0]
        updated = (source.astype(jnp.float32) + branch).astype(jnp.bfloat16)
        send_enc = jnp.where(encoder, updated, enc_full)
        send_dec = jnp.where(encoder, dec_full, updated)
        out_piece = cut_share(updated)
        for slot_id in range(batch_count):
            out_slots[slot_id] = jnp.where(batch_id == slot_id, out_piece, out_slots[slot_id])
        stored.append(
            (
                enc_full,
                source,
                q_factor,
                m_factor,
                queries,
                q_head,
                key_all,
                value_all,
                k_head,
                same_doc,
                attended,
            )
        )
    saved_ticks = [jnp.stack(fields) for fields in zip(*stored)]
    zeros_grad = jnp.zeros((tok_rows, model_width), jnp.bfloat16)
    enc_slots = [zeros_grad for slot_id in range(batch_count)]
    dec_slots = [zeros_grad for slot_id in range(batch_count)]
    half_width = local_heads * HS
    for tick_id in range(tick_count):
        batch_id = tick_id - (section_count - 1 - section_id)
        fwd_tick = jnp.clip(batch_id + section_id, 0, tick_count - 1)
        if tick_id > 0:
            grad_enc, grad_dec = shifted((back_enc, back_dec), "pipe", -1)
        else:
            grad_enc = zeros_grad
            grad_dec = zeros_grad
        if tick_id < batch_count:
            start_grad = out_grad[tick_id]
            grad_dec = jnp.where(section_id == section_count - 1, start_grad, grad_dec)
        full_enc, full_dec = (grad_enc, grad_dec)
        picked = [
            lax.dynamic_index_in_dim(fields, fwd_tick, 0, keepdims=False) for fields in saved_ticks
        ]
        (
            enc_full,
            source,
            q_factor,
            m_factor,
            queries,
            q_head,
            key_all,
            value_all,
            k_head,
            same_doc,
            attended,
        ) = picked
        upstream = jnp.where(encoder, full_enc, full_dec)
        d_attended = jnp.einsum("td,cd->tc", upstream, out_map, preferred_element_type=jnp.float32)
        d_attended = d_attended.astype(jnp.bfloat16).reshape(tok_rows, local_heads, HS)
        weights, totals = attend_keys(queries, key_all, same_doc, score_scale)
        portion = weights / totals[:, :, None]
        portion_low = portion.astype(jnp.bfloat16)
        along_values = jnp.einsum(
            "thd,khd->htk", d_attended, value_all, preferred_element_type=jnp.float32
        )
        delta_rows = jnp.sum(d_attended.astype(jnp.float32) * attended.astype(jnp.float32), axis=-1)
        d_scores = (portion * (along_values - jnp.transpose(delta_rows)[:, :, None])).astype(
            jnp.bfloat16
        )
        d_queries = (
            jnp.einsum("htk,khd->thd", d_scores, key_all, preferred_element_type=jnp.float32)
            * score_scale
        )
        row_count = tok_rows * lax.axis_size("seq")
        value_term = jnp.einsum(
            "htk,thd->khd", portion_low, d_attended, preferred_element_type=jnp.float32
        )
        key_term = (
            jnp.einsum("htk,thd->khd", d_scores, queries, preferred_element_type=jnp.float32)
            * score_scale
        )
        key_sums = lax.psum_scatter(
            jnp.concatenate(
                [value_term.reshape(row_count, -1), key_term.reshape(row_count, -1)], 1
            ).astype(jnp.bfloat16),
            "seq",
            scatter_dimension=0,
            tiled=True,
        ).astype(jnp.float32)
        d_values = key_sums[:, :half_width].astype(jnp.bfloat16)
        d_keys = key_sums[:, half_width:].reshape(tok_rows, local_heads, HS)
        key_local = lax.dynamic_slice_in_dim(key_all, seq_index * tok_rows, tok_rows, 0)
        q_grad = head_back(queries, q_head, d_queries).astype(jnp.bfloat16).reshape(tok_rows, -1)
        k_grad = head_back(key_local, k_head, d_keys).astype(jnp.bfloat16).reshape(tok_rows, -1)
        d_query_in = jnp.einsum("tc,dc->td", q_grad, query_map, preferred_element_type=jnp.float32)
        d_memory_in = jnp.einsum("tc,dc->td", k_grad, key_map, preferred_element_type=jnp.float32)
        d_memory_in = d_memory_in + jnp.einsum(
            "tc,dc->td", d_values, value_map, preferred_element_type=jnp.float32
        )
        both_sums = head_total(jnp.stack([d_query_in, d_memory_in]))
        back_q = norm_back(source, q_factor, stream_gain, both_sums[0])
        back_m = norm_back(enc_full, m_factor, stream_gain, both_sums[1])
        back_enc = (grad_enc.astype(jnp.float32) + back_m + jnp.where(encoder, back_q, 0.0)).astype(
            jnp.bfloat16
        )
        back_dec = (grad_dec.astype(jnp.float32) + jnp.where(encoder, 0.0, back_q)).astype(
            jnp.bfloat16
        )
        for slot_id in range(batch_count):
            matches = batch_id == slot_id
            enc_slots[slot_id] = jnp.where(matches, back_enc, enc_slots[slot_id])
            dec_slots[slot_id] = jnp.where(matches, back_dec, dec_slots[slot_id])
    section_out = jnp.stack(out_slots)[None]
    grad_stack = jnp.stack([jnp.stack(enc_slots), jnp.stack(dec_slots)])
    grad_stack = cut_share(grad_stack)
    section_grad = grad_stack[None]
    return (section_out, section_grad)


def solution(mesh):
    return jax.shard_map(
        per_device,
        mesh=mesh,
        in_specs=(
            P(None, "seq", None),
            P(None, "seq", None),
            P(),
            P(),
            P("pipe", None),
            P("pipe", None, "mp"),
            P("pipe", None, "mp"),
            P("pipe", None, "mp"),
            P("pipe", "mp", None),
            P(None, "seq", None),
        ),
        out_specs=(P("pipe", None, "seq", "mp"), P("pipe", None, None, "seq", "mp")),
        check_vma=False,
    )
```

profile of v0, /device:TPU:0, one launch (start us, length us, event | category | flops | bytes accessed | tf_op | source)
XLA Modules:
  0.0 899.2 jit_solution(279684312541402062)
XLA Ops:
  7.9 6.5 copy.94
  14.9 3.7 multiply_reduce_fusion.10
  18.7 5.9 all_gather.31
  24.5 6.5 copy.93
  31.1 3.7 multiply_reduce_fusion.11
  34.9 3.2 fusion.75
  38.1 4.9 all_gather.30
  46.1 2.3 constant_dynamic-update-slice_fusion.36
  56.2 30.0 %all-reduce.11.cloned.1.call-done = bf16[64,4096]{1,0:T(8,128)(2,1)} async-done(((bf16[64,4096]{1,0:T(8,128)(2,1)}), bf16[64,4096]{1,0:T(8,128)(2,1)}) %all-reduce.11.cloned.1.call-update) | async-done | bytes 524304 | tf_op jit(solution)/shard_map/psum | solution.py:54
  91.7 2.4 fusion.90
  94.1 4.4 collective-permute-start.1
  100.6 5.6 all_gather.32
  111.0 4.9 all_gather.33
  124.2 34.7 %all-reduce.13.cloned.1.call-done = bf16[64,4096]{1,0:T(8,128)(2,1)} async-done(((bf16[64,4096]{1,0:T(8,128)(2,1)}), bf16[64,4096]{1,0:T(8,128)(2,1)}) %all-reduce.13.cloned.1.call-update) | async-done | bytes 524304 | tf_op jit(solution)/shard_map/psum | solution.py:54
  164.4 4.3 collective-permute-start.3
  169.9 5.1 all_gather.34
  180.5 5.3 all_gather.35
  194.0 36.2 %all-reduce.15.cloned.1.call-done = bf16[64,4096]{1,0:T(8,128)(2,1)} async-done(((bf16[64,4096]{1,0:T(8,128)(2,1)}), bf16[64,4096]{1,0:T(8,128)(2,1)}) %all-reduce.15.cloned.1.call-update) | async-done | bytes 524304 | tf_op jit(solution)/shard_map/psum | solution.py:54
  236.9 4.1 collective-permute-start.5
  242.2 5.5 all_gather.36
  253.3 4.9 all_gather.37
  266.4 35.0 %all-reduce.17.cloned.1.call-done = bf16[64,4096]{1,0:T(8,128)(2,1)} async-done(((bf16[64,4096]{1,0:T(8,128)(2,1)}), bf16[64,4096]{1,0:T(8,128)(2,1)}) %all-reduce.17.cloned.1.call-update) | async-done | bytes 524304 | tf_op jit(solution)/shard_map/psum | solution.py:54
  304.6 4.5 collective-permute-start.7
  318.4 4.9 all_gather.39
  324.2 1.8 fusion.425
  327.8 3.1 fusion.87
  330.9 4.9 all_gather.38
  343.6 1.8 convolution_convert_fusion.14
  350.6 1.9 dynamic-slice_convert_fusion.1
  357.9 4.4 fusion.10
  362.3 7.1 reduce-scatter.6.cloned.1.call-done
  371.6 3.9 fusion.36
  380.1 49.9 %all-reduce.19.cloned.1.call-done = bf16[2,64,4096]{2,1,0:T(8,128)(2,1)} async-done(((bf16[2,64,4096]{2,1,0:T(8,128)(2,1)}), bf16[2,64,4096]{2,1,0:T(8,128)(2,1)}) %all-reduce.19.cloned.1.call-update) | async-done | bytes 1048592 | tf_op jit(solution)/shard_map/psum | solution.py:54
  433.0 2.6 fusion.240
  443.5 4.1 fusion.93
  452.8 1.8 convolution_convert_fusion.13
  460.9 4.4 fusion.11
  465.3 12.9 %reduce-scatter.8.cloned.1.call-done = bf16[64,1024]{1,0:T(8,128)(2,1)} async-done(((bf16[128,1024]{1,0:T(8,128)(2,1)}), bf16[64,1024]{1,0:T(8,128)(2,1)}) %reduce-scatter.8.cloned.1.call-update) | async-done | bytes 131088 | tf_op jit(solution)/shard_map/reduce_scatter | solution.py:219
  480.4 3.9 fusion.34
  486.8 51.9 %all-reduce.21.cloned.1.call-done = bf16[2,64,4096]{2,1,0:T(8,128)(2,1)} async-done(((bf16[2,64,4096]{2,1,0:T(8,128)(2,1)}), bf16[2,64,4096]{2,1,0:T(8,128)(2,1)}) %all-reduce.21.cloned.1.call-update) | async-done | bytes 1048592 | tf_op jit(solution)/shard_map/psum | solution.py:54
  541.8 3.3 add_convert_fusion.3
  549.3 1.8 fusion.419
  552.9 3.7 fusion.96
  561.9 1.8 convolution_convert_fusion.12
  569.8 4.4 fusion.12
  574.2 13.1 %reduce-scatter.10.cloned.1.call-done = bf16[64,1024]{1,0:T(8,128)(2,1)} async-done(((bf16[128,1024]{1,0:T(8,128)(2,1)}), bf16[64,1024]{1,0:T(8,128)(2,1)}) %reduce-scatter.10.cloned.1.call-update) | async-done | bytes 131088 | tf_op jit(solution)/shard_map/reduce_scatter | solution.py:219
  589.4 3.9 fusion.32
  595.9 51.9 %all-reduce.23.cloned.1.call-done = bf16[2,64,4096]{2,1,0:T(8,128)(2,1)} async-done(((bf16[2,64,4096]{2,1,0:T(8,128)(2,1)}), bf16[2,64,4096]{2,1,0:T(8,128)(2,1)}) %all-reduce.23.cloned.1.call-update) | async-done | bytes 1048592 | tf_op jit(solution)/shard_map/psum | solution.py:54
  650.8 3.2 add_convert_fusion.2
  658.5 1.8 fusion.416
  662.0 3.7 fusion.99
  671.0 1.8 convolution_convert_fusion.11
  679.0 4.4 fusion.13
  683.4 12.9 %reduce-scatter.12.cloned.1.call-done = bf16[64,1024]{1,0:T(8,128)(2,1)} async-done(((bf16[128,1024]{1,0:T(8,128)(2,1)}), bf16[64,1024]{1,0:T(8,128)(2,1)}) %reduce-scatter.12.cloned.1.call-update) | async-done | bytes 131088 | tf_op jit(solution)/shard_map/reduce_scatter | solution.py:219
  698.4 3.9 fusion.30
  708.2 1.8 fusion.413
  710.0 46.7 %all-reduce.25.cloned.1.call-done = bf16[2,64,4096]{2,1,0:T(8,128)(2,1)} async-done(((bf16[2,64,4096]{2,1,0:T(8,128)(2,1)}), bf16[2,64,4096]{2,1,0:T(8,128)(2,1)}) %all-reduce.25.cloned.1.call-update) | async-done | bytes 1048592 | tf_op jit(solution)/shard_map/psum | solution.py:54
  759.9 2.2 add_convert_fusion.1
  774.8 1.8 convolution_convert_fusion.10
  783.0 4.5 fusion.14
  787.5 14.2 %reduce-scatter.14.cloned.1.call-done = bf16[64,1024]{1,0:T(8,128)(2,1)} async-done(((bf16[128,1024]{1,0:T(8,128)(2,1)}), bf16[64,1024]{1,0:T(8,128)(2,1)}) %reduce-scatter.14.cloned.1.call-update) | async-done | bytes 131088 | tf_op jit(solution)/shard_map/reduce_scatter | solution.py:219
  806.6 3.8 fusion.38
  813.0 69.5 %all-reduce.27.cloned.1.call-done = (bf16[64,4096]{1,0:T(8,128)(2,1)}, bf16[2,64,4096]{2,1,0:T(8,128)(2,1)}) async-done(((bf16[64,4096]{1,0:T(8,128)(2,1)}, bf16[2,64,4096]{2,1,0:T(8,128)(2,1)}), (bf16[64,4096]{1,0:T(8,128)(2,1)}, bf16[2,64,4096]{2,1,0:T(8,128)(2,1)})) %all-reduce.27.cloned.1.call-update) | async-done | bytes 1572880 | tf_op jit(solution)/shard_map/psum | solution.py:54
  886.7 2.1 select_bitcast_fusion.3
  (614 shorter events, 230.3 us)
Async XLA Ops:
  7.2 79.1 %all-reduce.11.cloned.1.call-start = ((), (), s32[]{:S(2)}) async-start(), calls=%async_computation.5 | async-start | bytes 1048576 | tf_op jit(solution)/shard_map/psum | solution.py:54
  24.5 18.7 %copy-start.53 = (bf16[128,2,256]{2,0,1:T(8,128)(2,1)}, bf16[128,2,256]{2,0,1:T(8,128)(2,1)S(1)}, u32[]{:S(2)}) copy-start(bf16[128,2,256]{2,0,1:T(8,128)(2,1)S(1)} %all_gather.31) | copy-start | bytes 393220
  34.8 11.2 %copy-start.71 = (f32[64,2,256]{2,0,1:T(8,128)}, f32[64,2,256]{2,0,1:T(8,128)S(1)}, u32[]{:S(2)}) copy-start(f32[64,2,256]{2,0,1:T(8,128)S(1)} %get-tuple-element.95) | copy-start | bytes 393220
  34.8 9.5 %copy-start = (bf16[1,512,4096]{2,1,0:T(8,128)(2,1)S(1)}, bf16[1,512,4096]{2,1,0:T(8,128)(2,1)}, u32[]{:S(2)}) copy-start(bf16[1,512,4096]{2,1,0:T(8,128)(2,1)} %param.18) | copy-start | bytes 12582916
  43.5 11.4 %copy-start.54 = (bf16[128,2,256]{2,0,1:T(8,128)(2,1)S(1)}, bf16[128,2,256]{2,0,1:T(8,128)(2,1)}, u32[]{:S(2)}) copy-start(bf16[128,2,256]{2,0,1:T(8,128)(2,1)} %copy-done.53) | copy-start | bytes 393220
  46.0 112.9 %all-reduce.13.cloned.1.call-start = ((), (), s32[]{:S(2)}) async-start(), calls=%async_computation.6 | async-start | bytes 1048576 | tf_op jit(solution)/shard_map/psum | solution.py:54
  86.2 12.3 %copy-start.22 = (bf16[2,64,4096]{2,1,0:T(8,128)(2,1)S(1)}, bf16[2,64,4096]{2,1,0:T(8,128)(2,1)}, u32[]{:S(2)}) copy-start(bf16[2,64,4096]{2,1,0:T(8,128)(2,1)} %param.10) | copy-start | bytes 3145732
  87.9 11.7 %copy-start.5 = (bf16[1,4096,512]{2,1,0:T(8,128)(2,1)S(1)}, bf16[1,4096,512]{2,1,0:T(8,128)(2,1)}, u32[]{:S(2)}) copy-start(bf16[1,4096,512]{2,1,0:T(8,128)(2,1)} %param.17) | copy-start | bytes 12582916
  89.6 8.9 collective-permute-start
  94.1 12.2 %copy-start.13 = (bf16[512,4096]{1,0:T(8,128)(2,1)S(1)}, bf16[512,4096]{1,0:T(8,128)(2,1)}, u32[]{:S(2)}) copy-start(bf16[512,4096]{1,0:T(8,128)(2,1)} %copy.94) | copy-start | bytes 12582916
  94.1 13.7 %collective-permute-start.1 = (bf16[64,4096]{1,0:T(8,128)(2,1)S(1)}, bf16[64,4096]{1,0:T(8,128)(2,1)S(1)}, u32[]{:S(2)}, u32[]{:S(2)}) collective-permute-start(bf16[64,4096]{1,0:T(8,128)(2,1)S(1)} %get-tuple-element.36), channel_id=1, source_target_pairs={{0,8},{8,16},{16,24},{1,9},{9,17},{17,25},{2,10},{10,18},{18,26},{... | collective-permute-start | bytes 1572872 | tf_op jit(solution)/shard_map/ppermute | solution.py:16
  106.3 10.6 %copy-start.76 = (bf16[128,2,256]{2,0,1:T(8,128)(2,1)}, bf16[128,2,256]{2,0,1:T(8,128)(2,1)S(1)}, u32[]{:S(2)}) copy-start(bf16[128,2,256]{2,0,1:T(8,128)(2,1)S(1)} %all_gather.32) | copy-start | bytes 393220
  119.4 110.9 %all-reduce.15.cloned.1.call-start = ((), (), s32[]{:S(2)}) async-start(), calls=%async_computation.7 | async-start | bytes 1048576 | tf_op jit(solution)/shard_map/psum | solution.py:54
  159.0 10.0 %copy-start.6 = (bf16[1,4096,512]{2,1,0:T(8,128)(2,1)S(1)}, bf16[1,4096,512]{2,1,0:T(8,128)(2,1)}, u32[]{:S(2)}) copy-start(bf16[1,4096,512]{2,1,0:T(8,128)(2,1)} %param.17) | copy-start | bytes 12582916
  160.8 15.2 %copy-start.38 = (bf16[64,4096]{1,0:T(8,128)(2,1)}, bf16[64,4096]{1,0:T(8,128)(2,1)S(1)}, u32[]{:S(2)}) copy-start(bf16[64,4096]{1,0:T(8,128)(2,1)S(1)} %get-tuple-element.35) | copy-start | bytes 1572868
  160.8 7.8 collective-permute-start.2
  164.4 10.5 %collective-permute-start.3 = (bf16[64,4096]{1,0:T(8,128)(2,1)S(1)}, bf16[64,4096]{1,0:T(8,128)(2,1)S(1)}, u32[]{:S(2)}, u32[]{:S(2)}) collective-permute-start(bf16[64,4096]{1,0:T(8,128)(2,1)S(1)} %get-tuple-element.34), channel_id=1, source_target_pairs={{0,8},{8,16},{16,24},{1,9},{9,17},{17,25},{2,10},{10,18},{18,26},{... | collective-permute-start | bytes 1572872 | tf_op jit(solution)/shard_map/ppermute | solution.py:16
  174.9 11.8 %copy-start.74 = (bf16[128,2,256]{2,0,1:T(8,128)(2,1)}, bf16[128,2,256]{2,0,1:T(8,128)(2,1)S(1)}, u32[]{:S(2)}) copy-start(bf16[128,2,256]{2,0,1:T(8,128)(2,1)S(1)} %all_gather.34) | copy-start | bytes 393220
  176.8 9.7 %copy-start.90 = (pred[64,128]{1,0:T(8,128)(4,1)S(1)}, pred[64,128]{1,0:T(8,128)(4,1)}, u32[]{:S(2)}) copy-start(pred[64,128]{1,0:T(8,128)(4,1)} %broadcast_compare_fusion.2) | copy-start | bytes 24580
  189.3 112.1 %all-reduce.17.cloned.1.call-start = ((), (), s32[]{:S(2)}) async-start(), calls=%async_computation.8 | async-start | bytes 1048576 | tf_op jit(solution)/shard_map/psum | solution.py:54
  230.2 11.1 %copy-start.7 = (bf16[1,4096,512]{2,1,0:T(8,128)(2,1)S(1)}, bf16[1,4096,512]{2,1,0:T(8,128)(2,1)}, u32[]{:S(2)}) copy-start(bf16[1,4096,512]{2,1,0:T(8,128)(2,1)} %param.17) | copy-start | bytes 12582916
  232.0 9.0 %collective-permute-start.4 = (bf16[64,4096]{1,0:T(8,128)(2,1)S(1)}, bf16[64,4096]{1,0:T(8,128)(2,1)S(1)}, u32[]{:S(2)}, u32[]{:S(2)}) collective-permute-start(bf16[64,4096]{1,0:T(8,128)(2,1)S(1)} %broadcast_select_fusion.6), channel_id=1, source_target_pairs={{0,8},{8,16},{16,24},{1,9},{9,17},{17,25},{2,10},{10,18},{18,26},{... | collective-permute-start | bytes 1572872 | tf_op jit(solution)/shard_map/ppermute | solution.py:16
  236.9 10.8 %collective-permute-start.5 = (bf16[64,4096]{1,0:T(8,128)(2,1)S(1)}, bf16[64,4096]{1,0:T(8,128)(2,1)S(1)}, u32[]{:S(2)}, u32[]{:S(2)}) collective-permute-start(bf16[64,4096]{1,0:T(8,128)(2,1)S(1)} %get-tuple-element.32), channel_id=1, source_target_pairs={{0,8},{8,16},{16,24},{1,9},{9,17},{17,25},{2,10},{10,18},{18,26},{... | collective-permute-start | bytes 1572872 | tf_op jit(solution)/shard_map/ppermute | solution.py:16
  242.2 9.5 %copy-start.15 = (bf16[512,4096]{1,0:T(8,128)(2,1)S(1)}, bf16[512,4096]{1,0:T(8,128)(2,1)}, u32[]{:S(2)}) copy-start(bf16[512,4096]{1,0:T(8,128)(2,1)} %copy.94) | copy-start | bytes 12582916
  247.8 11.5 %copy-start.72 = (bf16[128,2,256]{2,0,1:T(8,128)(2,1)}, bf16[128,2,256]{2,0,1:T(8,128)(2,1)S(1)}, u32[]{:S(2)}) copy-start(bf16[128,2,256]{2,0,1:T(8,128)(2,1)S(1)} %all_gather.36) | copy-start | bytes 393220
  261.8 107.7 %reduce-scatter.6.cloned.1.call-start = ((), (), s32[]{:S(2)}) async-start(), calls=%async_computation.9 | async-start | bytes 393216 | tf_op jit(solution)/shard_map/reduce_scatter | solution.py:219
  301.3 10.6 %copy-start.73 = (bf16[128,2,256]{2,0,1:T(8,128)(2,1)S(1)}, bf16[128,2,256]{2,0,1:T(8,128)(2,1)}, u32[]{:S(2)}) copy-start(bf16[128,2,256]{2,0,1:T(8,128)(2,1)} %copy-done.72) | copy-start | bytes 393220
  301.3 13.1 %copy-start.20 = (bf16[512,4096]{1,0:T(8,128)(2,1)S(1)}, bf16[512,4096]{1,0:T(8,128)(2,1)}, u32[]{:S(2)}) copy-start(bf16[512,4096]{1,0:T(8,128)(2,1)} %copy.93) | copy-start | bytes 12582916
  303.1 9.6 %copy-start.40 = (bf16[64,4096]{1,0:T(8,128)(2,1)}, bf16[64,4096]{1,0:T(8,128)(2,1)S(1)}, u32[]{:S(2)}) copy-start(bf16[64,4096]{1,0:T(8,128)(2,1)S(1)} %get-tuple-element.31) | copy-start | bytes 1572868
  303.2 9.5 %collective-permute-start.6 = (bf16[64,4096]{1,0:T(8,128)(2,1)S(1)}, bf16[64,4096]{1,0:T(8,128)(2,1)S(1)}, u32[]{:S(2)}, u32[]{:S(2)}) collective-permute-start(bf16[64,4096]{1,0:T(8,128)(2,1)S(1)} %broadcast_select_fusion.3), channel_id=1, source_target_pairs={{0,8},{8,16},{16,24},{1,9},{9,17},{17,25},{2,10},{10,18},{18,26},{... | collective-permute-start | bytes 1572872 | tf_op jit(solution)/shard_map/ppermute | solution.py:16
  304.6 8.0 collective-permute-start.7
  326.0 9.9 %copy-start.63 = (f32[64,2,256]{2,0,1:T(8,128)S(1)}, f32[64,2,256]{2,0,1:T(8,128)}, u32[]{:S(2)}) copy-start(f32[64,2,256]{2,0,1:T(8,128)} %copy-done.62) | copy-start | bytes 393220
  326.0 9.9 %copy-start.65 = (bf16[128,2,256]{2,0,1:T(8,128)(2,1)S(1)}, bf16[128,2,256]{2,0,1:T(8,128)(2,1)}, u32[]{:S(2)}) copy-start(bf16[128,2,256]{2,0,1:T(8,128)(2,1)} %copy-done.64) | copy-start | bytes 393220
  326.0 9.9 %copy-start.88 = (pred[64,128]{1,0:T(8,128)(4,1)S(1)}, pred[64,128]{1,0:T(8,128)(4,1)}, u32[]{:S(2)}) copy-start(pred[64,128]{1,0:T(8,128)(4,1)} %broadcast_compare_fusion) | copy-start | bytes 24580
  326.0 9.9 %copy-start.101 = (f32[64,2]{0,1:T(2,128)S(1)}, f32[64,2]{0,1:T(2,128)}, u32[]{:S(2)}) copy-start(f32[64,2]{0,1:T(2,128)} %copy-done.100) | copy-start | bytes 1540
  326.0 12.6 %copy-start.84 = (f32[2,64,128]{2,1,0:T(8,128)S(1)}, f32[2,64,128]{2,1,0:T(8,128)}, u32[]{:S(2)}) copy-start(f32[2,64,128]{2,1,0:T(8,128)} %fusion.425) | copy-start | bytes 196612
  326.0 15.7 %copy-start.135 = (f32[64]{0:T(128)S(1)}, f32[64]{0:T(128)}, u32[]{:S(2)}) copy-start(f32[64]{0:T(128)} %copy-done.134) | copy-start | bytes 772
  326.0 16.2 %copy-start.25 = (bf16[64,4096]{1,0:T(8,128)(2,1)S(1)}, bf16[64,4096]{1,0:T(8,128)(2,1)}, u32[]{:S(2)}) copy-start(bf16[64,4096]{1,0:T(8,128)(2,1)} %copy-done.24) | copy-start | bytes 1572868
  327.8 14.5 %copy-start.104 = (f32[64,2]{0,1:T(2,128)S(1)}, f32[64,2]{0,1:T(2,128)}, u32[]{:S(2)}) copy-start(f32[64,2]{0,1:T(2,128)} %copy-done.103) | copy-start | bytes 1540
  327.8 14.5 %copy-start.111 = (f32[5,64,2,1]{1,2,3,0:T(2,128)S(1)}, f32[5,64,2,1]{1,2,3,0:T(2,128)}, u32[]{:S(2)}) copy-start(f32[5,64,2,1]{1,2,3,0:T(2,128)} %constant_dynamic-update-slice_fusion.6) | copy-start | bytes 7684
  350.5 79.4 %all-reduce.19.cloned.1.call-start = ((), (), s32[]{:S(2)}) async-start(), calls=%async_computation.10 | async-start | bytes 2097152 | tf_op jit(solution)/shard_map/psum | solution.py:54
  378.0 100.2 %reduce-scatter.8.cloned.1.call-start = ((), (), s32[]{:S(2)}) async-start(), calls=%async_computation.11 | async-start | bytes 393216 | tf_op jit(solution)/shard_map/reduce_scatter | solution.py:219
  435.7 7.8 collective-permute-start.8
  437.0 6.5 collective-permute-start.9
  459.7 79.0 %all-reduce.21.cloned.1.call-start = ((), (), s32[]{:S(2)}) async-start(), calls=%async_computation.12 | async-start | bytes 2097152 | tf_op jit(solution)/shard_map/psum | solution.py:54
  486.7 55.1 %copy-start.119 = (f32[64]{0:T(128)S(1)}, f32[64]{0:T(128)}, u32[]{:S(2)}) copy-start(f32[64]{0:T(128)} %get-tuple-element.75) | copy-start | bytes 772
  486.7 55.1 %copy-start.120 = (f32[64]{0:T(128)S(1)}, f32[64]{0:T(128)}, u32[]{:S(2)}) copy-start(f32[64]{0:T(128)} %get-tuple-element.80) | copy-start | bytes 772
  486.7 100.6 %reduce-scatter.10.cloned.1.call-start = ((), (), s32[]{:S(2)}) async-start(), calls=%async_computation.13 | async-start | bytes 393216 | tf_op jit(solution)/shard_map/reduce_scatter | solution.py:219
  545.1 7.8 collective-permute-start.10
  546.4 6.5 collective-permute-start.11
  568.8 79.0 %all-reduce.23.cloned.1.call-start = ((), (), s32[]{:S(2)}) async-start(), calls=%async_computation.14 | async-start | bytes 2097152 | tf_op jit(solution)/shard_map/psum | solution.py:54
  595.8 55.0 %copy-start.124 = (f32[64]{0:T(128)S(1)}, f32[64]{0:T(128)}, u32[]{:S(2)}) copy-start(f32[64]{0:T(128)} %get-tuple-element.74) | copy-start | bytes 772
  595.8 55.0 %copy-start.125 = (f32[64]{0:T(128)S(1)}, f32[64]{0:T(128)}, u32[]{:S(2)}) copy-start(f32[64]{0:T(128)} %get-tuple-element.79) | copy-start | bytes 772
  595.8 100.4 %reduce-scatter.12.cloned.1.call-start = ((), (), s32[]{:S(2)}) async-start(), calls=%async_computation.15 | async-start | bytes 393216 | tf_op jit(solution)/shard_map/reduce_scatter | solution.py:219
  654.0 8.0 collective-permute-start.12
  655.3 6.7 collective-permute-start.13
  677.9 78.8 %all-reduce.25.cloned.1.call-start = ((), (), s32[]{:S(2)}) async-start(), calls=%async_computation.16 | async-start | bytes 2097152 | tf_op jit(solution)/shard_map/psum | solution.py:54
  704.8 96.9 %reduce-scatter.14.cloned.1.call-start = ((), (), s32[]{:S(2)}) async-start(), calls=%async_computation.17 | async-start | bytes 393216 | tf_op jit(solution)/shard_map/reduce_scatter | solution.py:219
  762.1 6.0 collective-permute-start.14
  763.4 4.7 collective-permute-start.15
  781.6 100.9 %all-reduce.27.cloned.1.call-start = ((), (), s32[]{:S(2)}) async-start(), calls=%async_computation.18 | async-start | bytes 3145728 | tf_op jit(solution)/shard_map/psum | solution.py:54
  783.0 23.6 %copy-start.68 = (f32[8,8,2,256]{3,1,2,0:T(8,128)S(1)}, f32[8,8,2,256]{3,1,2,0:T(8,128)}, u32[]{:S(2)}) copy-start(f32[8,8,2,256]{3,1,2,0:T(8,128)} %copy.133) | copy-start | bytes 393220
  783.0 23.6 %copy-start.70 = (f32[8,8,2,256]{3,1,2,0:T(8,128)S(1)}, f32[8,8,2,256]{3,1,2,0:T(8,128)}, u32[]{:S(2)}) copy-start(f32[8,8,2,256]{3,1,2,0:T(8,128)} %copy.132) | copy-start | bytes 393220
  812.9 72.6 %copy-start.112 = (f32[64]{0:T(128)S(1)}, f32[64]{0:T(128)}, u32[]{:S(2)}) copy-start(f32[64]{0:T(128)} %get-tuple-element.77) | copy-start | bytes 772
  (102 other events, 470.2 us)
Sparse Core Ops, SparseCore 0:
  46.1 40.0 all-reduce.10
  119.5 39.4 all-reduce.12
  189.4 40.8 all-reduce.14
  261.9 39.4 all-reduce.16
  350.6 18.7 reduce-scatter.5
  378.1 51.8 all-reduce.18
  459.8 18.3 reduce-scatter.7
  486.9 51.8 all-reduce.20
  568.9 18.3 reduce-scatter.9
  595.9 51.8 all-reduce.22
  678.0 18.1 reduce-scatter.11
  704.9 51.8 all-reduce.24
  781.8 19.8 reduce-scatter.13
  813.0 69.4 all-reduce.26
where the time goes:
time: 913 us; the launch traced here: 899 us
  waiting for transfers between devices  466 us (51%)
  matrix products  150 us (16%)
  other arithmetic  114 us (12%)
  local copies, waits for them, and re-layouts  64 us (7%)
  blocking collectives  52.2 us (6%)
  starting transfers between devices  34.8 us (4%)
  between operations  17.3 us (2%)
    psum x9, waiting for transfers between devices, head_total(): return lax.psum(values.astype(jnp.bfloat16), 'mp').astype(jnp.float32)  406 us
    reduce_scatter x5, waiting for transfers between devices, per_device(): lax.psum_scatter(jnp.concatenate([value_term.reshape(row_count, -1), key_...  60.2 us
    ppermute x16, starting transfers between devices, shifted(): return lax.ppermute(x, axis, pairs)  33.8 us
    unnamed x34, other arithmetic  30.4 us
    all_gather x5, blocking collectives, per_device(): lax.all_gather(value_rows, 'seq', axis=0, tiled=True)  26.1 us
    all_gather x5, blocking collectives, per_device(): lax.all_gather(key_rows, 'seq', axis=0, tiled=True)  26 us
    dot_general x5, matrix products, per_device(): jnp.einsum('tc,dc->td', q_grad, query_map, preferred_element_type=jnp.flo...  22 us
    unnamed x295, local copies, waits for them, and re-layouts  20.7 us
  transfers between devices with their start and end apart: 30, of which 14 were waited for; matrix products, arithmetic and copies ran while one was open for 11% of the time, Pallas kernels for 0%

commit v1 on v0

v1 whole, which is shorter than its diff:
```python
import functools

import jax
import jax.numpy as jnp
from jax import lax
from jax.experimental import pallas as pl
from jax.experimental.pallas import tpu as pltpu
from jax.sharding import PartitionSpec as P

HEADS = 8
HS = 256
PAD = 128

epsilon = 1e-06
MESH = pl.DeviceIdType.MESH
F32 = jnp.float32
BF16 = jnp.bfloat16


def dot_nn(a, b):
    return jnp.dot(a, b, preferred_element_type=F32)


def dot_nt(a, b):
    return lax.dot_general(a, b, (((1,), (1,)), ((), ())), preferred_element_type=F32)


def dot_tn(a, b):
    return lax.dot_general(a, b, (((0,), (0,)), ((), ())), preferred_element_type=F32)


def kernel(
    n_pipe,
    n_seq,
    n_mp,
    enc_ref,
    dec_ref,
    doc_ref,
    count_ref,
    gain_ref,
    wq_hbm,
    wk_hbm,
    wv_hbm,
    wo_hbm,
    og_ref,
    so_ref,
    sg_ref,
    wq,
    wk,
    wv,
    wo,
    w_sem,
    mask,
    upd_recv,
    enc_recv,
    enc_cur,
    src_cur,
    q_acc,
    k_acc,
    v_acc,
    queries,
    q_factor,
    m_factor,
    q_head,
    k_head,
    kv_all,
    portion,
    attended,
    fs_send,
    fs_recv,
    upd_send,
    u_recv,
    d_att,
    kvg_send,
    kvg_recv,
    q_grad,
    k_grad,
    v_grad,
    dq_buf,
    a_send,
    a_recv,
    b_send,
    b_recv,
    ahop,
    bhop,
    gb_recv,
    upd_ssem,
    upd_rsem,
    enc_ssem,
    enc_rsem,
    kv_ssem,
    kv_rsem,
    fs_ssem,
    fs_rsem,
    u_ssem,
    u_rsem,
    kvg_ssem,
    kvg_rsem,
    a_ssem,
    a_rsem,
    b_ssem,
    b_rsem,
    gb_ssem,
    gb_rsem,
):
    pipe = lax.axis_index("pipe")
    seq = lax.axis_index("seq")
    z = lax.axis_index("mp")
    batches, toks, width = enc_ref.shape
    rows = batches * toks
    share = width // n_mp
    heads = HEADS // n_mp
    units = heads * HS
    scale = HS ** (-0.5)
    last = n_pipe - 1

    def at_mp(j):
        return (pipe, seq, j)

    def at_seq(i):
        return (pipe, i, z)

    def copy(src, dst, ssem, rsem, device):
        return pltpu.make_async_remote_copy(
            src_ref=src,
            dst_ref=dst,
            send_sem=ssem,
            recv_sem=rsem,
            device_id=device,
            device_id_type=MESH,
        )

    weight_loads = [
        pltpu.make_async_copy(hbm.at[0], vmem, w_sem.at[i])
        for i, (hbm, vmem) in enumerate(
            [(wk_hbm, wk), (wv_hbm, wv), (wq_hbm, wq), (wo_hbm, wo)]
        )
    ]
    for load in weight_loads:
        load.start()

    barrier = pltpu.get_barrier_semaphore()
    for k in range(1, n_mp):
        pl.semaphore_signal(
            barrier, inc=1, device_id=at_mp(lax.rem(z + k, n_mp)), device_id_type=MESH
        )
    for k in range(1, n_seq):
        pl.semaphore_signal(
            barrier, inc=1, device_id=at_seq(lax.rem(seq + k, n_seq)), device_id_type=MESH
        )

    @pl.when(pipe > 0)
    def _():
        for j in range(n_mp):
            pl.semaphore_signal(
                barrier, inc=1, device_id=(pipe - 1, seq, j), device_id_type=MESH
            )

    @pl.when(pipe < last)
    def _():
        for j in range(n_mp):
            pl.semaphore_signal(
                barrier, inc=1, device_id=(pipe + 1, seq, j), device_id_type=MESH
            )

    edge = jnp.where(pipe > 0, n_mp, 0) + jnp.where(pipe < last, n_mp, 0)
    pl.semaphore_wait(barrier, n_mp - 1 + n_seq - 1 + edge)

    encoder = pipe < count_ref[0]
    prev_encoder = pipe - 1 < count_ref[0]

    def cut(ref, j):
        lanes = pl.ds(pl.multiple_of(j * share, share), share)
        return ref[:, :, lanes].reshape(rows, share)

    def gain_of(j):
        return gain_ref[:, pl.ds(pl.multiple_of(j * share, share), share)]

    def chunk_rows(ref, j):
        return ref[pl.ds(pl.multiple_of(j * share, share), share), :]

    def chunk_cols(ref, j):
        return ref[:, pl.ds(pl.multiple_of(j * share, share), share)]

    length = n_seq * toks
    for m in range(batches):
        row = doc_ref[m : m + 1, :].astype(F32)
        spread = jnp.broadcast_to(row, (length, length))
        mask[m] = (spread == spread.T).astype(F32)

    @pl.when(pipe == 0)
    def _():
        def fill(j, carry):
            upd_recv[j] = cut(enc_ref, j)
            return carry

        lax.fori_loop(0, n_mp, fill, 0)

    q_acc[...] = jnp.zeros_like(q_acc)
    k_acc[...] = jnp.zeros_like(k_acc)
    v_acc[...] = jnp.zeros_like(v_acc)
    for load in weight_loads[:3]:
        load.wait()

    @pl.when(pipe > 0)
    def _():
        copy(enc_cur, enc_recv, enc_ssem, enc_rsem, at_mp(z)).wait_recv()

    def project(k, sums):
        j = lax.rem(z + k, n_mp)

        @pl.when(pipe > 0)
        def _():
            copy(upd_send, upd_recv.at[j], upd_ssem.at[j], upd_rsem.at[j], at_mp(z)).wait_recv()

        fresh = upd_recv[j].astype(F32)
        enc = jnp.where(prev_encoder, fresh, enc_recv[j].astype(F32))
        dec = jnp.where(prev_encoder, cut(dec_ref, j).astype(F32), fresh)
        src = jnp.where(encoder, enc, dec)
        enc_cur[j] = enc.astype(BF16)
        src_cur[j] = src.astype(BF16)
        gain = gain_of(j)
        m_part = (enc * gain).astype(BF16)
        q_part = (src * gain).astype(BF16)
        k_acc[...] += dot_nn(m_part, chunk_rows(wk, j))
        v_acc[...] += dot_nn(m_part, chunk_rows(wv, j))
        q_acc[...] += dot_nn(q_part, chunk_rows(wq, j))
        return (
            sums[0] + jnp.sum(src * src, axis=-1, keepdims=True),
            sums[1] + jnp.sum(enc * enc, axis=-1, keepdims=True),
        )

    none = jnp.zeros((rows, 1), F32)
    q_square, m_square = lax.fori_loop(0, n_mp, project, (none, none))
    q_factor[...] = lax.rsqrt(q_square / width + epsilon)
    m_factor[...] = lax.rsqrt(m_square / width + epsilon)

    for h in range(heads):
        lanes = slice(h * HS, (h + 1) * HS)
        keys = k_acc[:, lanes] * m_factor[...]
        head = lax.rsqrt(jnp.mean(keys * keys, axis=-1, keepdims=True) + epsilon)
        k_head[h] = head
        kv_all[seq, :, lanes] = (keys * head).astype(BF16)
    kv_all[seq, :, units:] = (v_acc[...] * m_factor[...]).astype(BF16)
    kv_copies = []
    for k in range(1, n_seq):
        peer = lax.rem(seq + k, n_seq)
        moved = copy(
            kv_all.at[seq], kv_all.at[seq], kv_ssem.at[k], kv_rsem.at[seq], at_seq(peer)
        )
        moved.start()
        kv_copies.append(moved)

    @pl.when(pipe < last)
    def _():
        copy(enc_cur, enc_recv, enc_ssem, enc_rsem, (pipe + 1, seq, z)).start()

    for h in range(heads):
        lanes = slice(h * HS, (h + 1) * HS)
        found = q_acc[:, lanes] * q_factor[...]
        head = lax.rsqrt(jnp.mean(found * found, axis=-1, keepdims=True) + epsilon)
        q_head[h] = head
        queries[:, lanes] = (found * head).astype(BF16)

    for k in range(1, n_seq):
        peer = lax.rem(seq + k, n_seq)
        copy(
            kv_all.at[seq], kv_all.at[peer], kv_ssem.at[k], kv_rsem.at[peer], at_seq(peer)
        ).wait_recv()

    def keys_of(m, h):
        lanes = slice(h * HS, (h + 1) * HS)
        return kv_all[:, m * toks : (m + 1) * toks, lanes].reshape(length, HS)

    def values_of(m, h):
        lanes = slice(units + h * HS, units + (h + 1) * HS)
        return kv_all[:, m * toks : (m + 1) * toks, lanes].reshape(length, HS)

    my_rows = pl.ds(pl.multiple_of(seq * toks, toks), toks)
    for m in range(batches):
        span = slice(m * toks, (m + 1) * toks)
        same = mask[m, my_rows, :]
        for h in range(heads):
            lanes = slice(h * HS, (h + 1) * HS)
            scores = dot_nt(queries[span, lanes], keys_of(m, h)) * scale
            weights = jnp.exp(scores) * same
            totals = jnp.sum(weights, axis=-1, keepdims=True)
            summed = dot_nn(weights.astype(BF16), values_of(m, h))
            attended[span, lanes] = (summed / totals).astype(BF16)
            portion[m, h] = weights / totals

    weight_loads[3].wait()

    def emit(k, carry):
        j = lax.rem(z + 1 + k, n_mp)
        fs_send[j] = dot_nn(attended[...], chunk_cols(wo, j)).astype(BF16)

        @pl.when(k < n_mp - 1)
        def _():
            copy(fs_send.at[j], fs_recv.at[z], fs_ssem.at[j], fs_rsem.at[z], at_mp(j)).start()

        return carry

    lax.fori_loop(0, n_mp, emit, 0)
    branch = fs_send[z].astype(F32)
    for k in range(1, n_mp):
        j = lax.rem(z + k, n_mp)
        copy(fs_send.at[j], fs_recv.at[j], fs_ssem.at[j], fs_rsem.at[j], at_mp(j)).wait_recv()
        branch = branch + fs_recv[j].astype(F32)
    updated = (src_cur[z].astype(F32) + branch).astype(BF16)
    upd_send[...] = updated

    @pl.when(pipe < last)
    def _():
        for j in range(n_mp):
            copy(
                upd_send, upd_recv.at[z], upd_ssem.at[j], upd_rsem.at[z], (pipe + 1, seq, j)
            ).start()

    so_ref[0] = updated.reshape(batches, toks, share)

    @pl.when(pipe == last)
    def _():
        def fill(j, carry):
            start = cut(og_ref, j).astype(F32)
            u_recv[j] = jnp.where(encoder, 0.0, start).astype(BF16)
            return carry

        lax.fori_loop(0, n_mp, fill, 0)
        start = cut(og_ref, z).astype(F32)
        gb_recv[...] = jnp.where(encoder, start, 0.0).astype(BF16)

    def pull(k, total):
        j = lax.rem(z + k, n_mp)

        @pl.when(pipe < last)
        def _():
            copy(ahop, u_recv.at[j], u_ssem.at[j], u_rsem.at[j], at_mp(z)).wait_recv()

        return total + dot_nt(u_recv[j], chunk_cols(wo, j))

    d_att[...] = lax.fori_loop(0, n_mp, pull, jnp.zeros((rows, units), F32)).astype(BF16)

    q_stat = none
    for m in range(batches):
        span = slice(m * toks, (m + 1) * toks)
        for h in range(heads):
            lanes = slice(h * HS, (h + 1) * HS)
            wide = slice(units + h * HS, units + (h + 1) * HS)
            keys = keys_of(m, h)
            probs = portion[m, h]
            pulled = d_att[span, lanes]
            along = dot_nt(pulled, values_of(m, h))
            delta = jnp.sum(
                pulled.astype(F32) * attended[span, lanes].astype(F32), axis=-1, keepdims=True
            )
            d_scores = (probs * (along - delta)).astype(BF16)
            asked = queries[span, lanes]
            value_term = dot_tn(probs.astype(BF16), pulled)
            key_term = dot_tn(d_scores, asked) * scale
            kvg_send[:, span, lanes] = key_term.astype(BF16).reshape(n_seq, toks, HS)
            kvg_send[:, span, wide] = value_term.astype(BF16).reshape(n_seq, toks, HS)
            d_queries = dot_nn(d_scores, keys) * scale
            normed = asked.astype(F32)
            mean = jnp.mean(d_queries * normed, axis=-1, keepdims=True)
            q_grad[span, lanes] = (q_head[h, span, :] * (d_queries - normed * mean)).astype(BF16)

    for k in range(1, n_seq):
        peer = lax.rem(seq + k, n_seq)
        copy(
            kvg_send.at[peer], kvg_recv.at[seq], kvg_ssem.at[k], kvg_rsem.at[seq], at_seq(peer)
        ).start()

    q_stat = jnp.sum(q_grad[...].astype(F32) * q_acc[...], axis=-1, keepdims=True)

    def ask(k, carry):
        j = lax.rem(z + 1 + k, n_mp)
        dq_buf[j] = dot_nt(q_grad[...], chunk_rows(wq, j))
        return carry

    lax.fori_loop(0, n_mp, ask, 0)

    d_kv = kvg_send[seq].astype(F32)
    for k in range(1, n_seq):
        peer = lax.rem(seq + k, n_seq)
        copy(
            kvg_send.at[peer], kvg_recv.at[peer], kvg_ssem.at[k], kvg_rsem.at[peer], at_seq(peer)
        ).wait_recv()
        d_kv = d_kv + kvg_recv[peer].astype(F32)
    v_grad[...] = d_kv[:, units:].astype(BF16)
    for h in range(heads):
        lanes = slice(h * HS, (h + 1) * HS)
        d_keys = d_kv[:, lanes]
        normed = kv_all[seq, :, lanes].astype(F32)
        mean = jnp.mean(d_keys * normed, axis=-1, keepdims=True)
        k_grad[:, lanes] = (k_head[h] * (d_keys - normed * mean)).astype(BF16)
    m_stat = jnp.sum(
        k_grad[...].astype(F32) * k_acc[...] + v_grad[...].astype(F32) * v_acc[...],
        axis=-1,
        keepdims=True,
    )

    def sort_a(dq, dm):
        return jnp.where(encoder, dq + dm, jnp.where(prev_encoder, dm, dq))

    def sort_b(dq, dm):
        return jnp.where(encoder, 0.0, jnp.where(prev_encoder, dq, dm))

    a_stat = jnp.broadcast_to(sort_a(q_stat, m_stat), (rows, PAD)).astype(BF16)
    b_stat = jnp.broadcast_to(sort_b(q_stat, m_stat), (rows, PAD)).astype(BF16)

    def spread_out(k, carry):
        j = lax.rem(z + 1 + k, n_mp)
        dm = dot_nt(k_grad[...], chunk_rows(wk, j)) + dot_nt(v_grad[...], chunk_rows(wv, j))
        dq = dq_buf[j]
        a_send[j, :, :share] = sort_a(dq, dm).astype(BF16)
        a_send[j, :, share:] = a_stat

        @pl.when(k < n_mp - 1)
        def _():
            copy(a_send.at[j], a_recv.at[z], a_ssem.at[j], a_rsem.at[z], at_mp(j)).start()

        b_send[j, :, :share] = sort_b(dq, dm).astype(BF16)
        b_send[j, :, share:] = b_stat
        return carry

    lax.fori_loop(0, n_mp, spread_out, 0)

    gain = gain_of(z)
    enc_share = enc_cur[z].astype(F32)
    src_share = src_cur[z].astype(F32)
    own = u_recv[z].astype(F32)

    def norm_back(values, factor, total):
        body = total[:, :share]
        stat = total[:, share : share + 1]
        return factor * (gain * body - values * (factor * factor * (stat / width)))

    total = a_send[z].astype(F32)
    for k in range(1, n_mp):
        j = lax.rem(z + k, n_mp)
        copy(a_send.at[j], a_recv.at[j], a_ssem.at[j], a_rsem.at[j], at_mp(j)).wait_recv()
        total = total + a_recv[j].astype(F32)

    @pl.when(pipe < last)
    def _():
        copy(bhop, gb_recv, gb_ssem, gb_rsem, at_mp(z)).wait_recv()

    other = gb_recv[...].astype(F32)
    turns = jnp.logical_and(jnp.logical_not(encoder), prev_encoder)
    a_values = jnp.where(turns, enc_share, src_share)
    a_factor = jnp.where(turns, m_factor[...], q_factor[...])
    a_new = (jnp.where(turns, other, own) + norm_back(a_values, a_factor, total)).astype(BF16)
    ahop[...] = a_new

    @pl.when(pipe > 0)
    def _():
        for j in range(n_mp):
            copy(ahop, u_recv.at[z], u_ssem.at[j], u_rsem.at[z], (pipe - 1, seq, j)).start()
        for j in range(n_mp):
            copy(ahop, u_recv.at[z], u_ssem.at[j], u_rsem.at[z], (pipe - 1, seq, j)).wait_send()

    for k in range(1, n_mp):
        j = lax.rem(z + k, n_mp)
        copy(b_send.at[j], b_recv.at[z], b_ssem.at[j], b_rsem.at[z], at_mp(j)).start()
    total = b_send[z].astype(F32)
    for k in range(1, n_mp):
        j = lax.rem(z + k, n_mp)
        copy(b_send.at[j], b_recv.at[j], b_ssem.at[j], b_rsem.at[j], at_mp(j)).wait_recv()
        total = total + b_recv[j].astype(F32)
    b_values = jnp.where(turns, src_share, enc_share)
    b_factor = jnp.where(turns, q_factor[...], m_factor[...])
    b_new = (jnp.where(turns, own, other) + norm_back(b_values, b_factor, total)).astype(BF16)
    bhop[...] = b_new

    @pl.when(pipe > 0)
    def _():
        copy(bhop, gb_recv, gb_ssem, gb_rsem, (pipe - 1, seq, z)).start()

    first = jnp.logical_or(encoder, prev_encoder)
    a_wide = a_new.astype(F32)
    b_wide = b_new.astype(F32)
    sg_ref[0, 0] = jnp.where(first, a_wide, b_wide).astype(BF16).reshape(batches, toks, share)
    sg_ref[0, 1] = jnp.where(first, b_wide, a_wide).astype(BF16).reshape(batches, toks, share)

    for moved in kv_copies:
        moved.wait_send()
    for k in range(1, n_seq):
        copy(
            kvg_send.at[seq], kvg_recv.at[seq], kvg_ssem.at[k], kvg_rsem.at[seq], at_seq(seq)
        ).wait_send()
    for k in range(1, n_mp):
        j = lax.rem(z + k, n_mp)
        copy(fs_send.at[j], fs_recv.at[z], fs_ssem.at[j], fs_rsem.at[z], at_mp(j)).wait_send()
        copy(a_send.at[j], a_recv.at[z], a_ssem.at[j], a_rsem.at[z], at_mp(j)).wait_send()
        copy(b_send.at[j], b_recv.at[z], b_ssem.at[j], b_rsem.at[z], at_mp(j)).wait_send()

    @pl.when(pipe < last)
    def _():
        copy(enc_cur, enc_recv, enc_ssem, enc_rsem, (pipe + 1, seq, z)).wait_send()
        for j in range(n_mp):
            copy(
                upd_send, upd_recv.at[z], upd_ssem.at[j], upd_rsem.at[z], (pipe + 1, seq, j)
            ).wait_send()

    @pl.when(pipe > 0)
    def _():
        copy(bhop, gb_recv, gb_ssem, gb_rsem, (pipe - 1, seq, z)).wait_send()


def per_device(n_pipe, n_seq, n_mp, enc_in, dec_in, doc_ids, enc_sections, norm_gain,
               q_weight, k_weight, v_weight, o_weight, out_grad):
    batches, toks, width = enc_in.shape
    rows = batches * toks
    share = width // n_mp
    heads = HEADS // n_mp
    units = heads * HS
    length = n_seq * toks
    vmem = pl.BlockSpec(memory_space=pltpu.VMEM)
    hbm = pl.BlockSpec(memory_space=pl.ANY)
    smem = pl.BlockSpec(memory_space=pltpu.SMEM)
    V = pltpu.VMEM
    dma = pltpu.SemaphoreType.DMA
    scratch = [
        V((width, units), BF16),
        V((width, units), BF16),
        V((width, units), BF16),
        V((units, width), BF16),
        dma((4,)),
        V((batches, length, length), F32),
        V((n_mp, rows, share), BF16),
        V((n_mp, rows, share), BF16),
        V((n_mp, rows, share), BF16),
        V((n_mp, rows, share), BF16),
        V((rows, units), F32),
        V((rows, units), F32),
        V((rows, units), F32),
        V((rows, units), BF16),
        V((rows, 1), F32),
        V((rows, 1), F32),
        V((heads, rows, 1), F32),
        V((heads, rows, 1), F32),
        V((n_seq, rows, 2 * units), BF16),
        V((batches, heads, toks, length), F32),
        V((rows, units), BF16),
        V((n_mp, rows, share), BF16),
        V((n_mp, rows, share), BF16),
        V((rows, share), BF16),
        V((n_mp, rows, share), BF16),
        V((rows, units), BF16),
        V((n_seq, rows, 2 * units), BF16),
        V((n_seq, rows, 2 * units), BF16),
        V((rows, units), BF16),
        V((rows, units), BF16),
        V((rows, units), BF16),
        V((n_mp, rows, share), F32),
        V((n_mp, rows, share + PAD), BF16),
        V((n_mp, rows, share + PAD), BF16),
        V((n_mp, rows, share + PAD), BF16),
        V((n_mp, rows, share + PAD), BF16),
        V((rows, share), BF16),
        V((rows, share), BF16),
        V((rows, share), BF16),
        dma((n_mp,)),
        dma((n_mp,)),
        dma,
        dma,
        dma((n_seq,)),
        dma((n_seq,)),
        dma((n_mp,)),
        dma((n_mp,)),
        dma((n_mp,)),
        dma((n_mp,)),
        dma((n_seq,)),
        dma((n_seq,)),
        dma((n_mp,)),
        dma((n_mp,)),
        dma((n_mp,)),
        dma((n_mp,)),
        dma,
        dma,
    ]
    return pl.pallas_call(
        functools.partial(kernel, n_pipe, n_seq, n_mp),
        out_shape=(
            jax.ShapeDtypeStruct((1, batches, toks, share), BF16),
            jax.ShapeDtypeStruct((1, 2, batches, toks, share), BF16),
        ),
        in_specs=[vmem, vmem, vmem, smem, vmem, hbm, hbm, hbm, hbm, vmem],
        out_specs=(vmem, vmem),
        scratch_shapes=scratch,
        compiler_params=pltpu.CompilerParams(
            collective_id=0, has_side_effects=True, vmem_limit_bytes=56 * 1024 * 1024
        ),
    )(enc_in, dec_in, doc_ids, enc_sections, norm_gain, q_weight, k_weight, v_weight, o_weight,
      out_grad)


def solution(mesh):
    sizes = (mesh.shape["pipe"], mesh.shape["seq"], mesh.shape["mp"])
    return jax.shard_map(
        functools.partial(per_device, *sizes),
        mesh=mesh,
        in_specs=(
            P(None, "seq", None),
            P(None, "seq", None),
            P(),
            P(),
            P("pipe", None),
            P("pipe", None, "mp"),
            P("pipe", None, "mp"),
            P("pipe", None, "mp"),
            P("pipe", "mp", None),
            P(None, "seq", None),
        ),
        out_specs=(P("pipe", None, "seq", "mp"), P("pipe", None, None, "seq", "mp")),
        check_vma=False,
    )
```

time: 913 us -> 295 us (0.32); the launches traced: 899 us -> 291 us
  waiting for transfers between devices: 466 us -> 0 us
  Pallas kernels: 0 us -> 287 us
  matrix products: 150 us -> 0 us
  other arithmetic: 114 us -> 0 us
  local copies, waits for them, and re-layouts: 64 us -> 3.54 us
  blocking collectives: 52.2 us -> 0 us
  starting transfers between devices: 34.8 us -> 0 us
  between operations: 17.3 us -> 1.29 us
    psum x9 -> x0, waiting for transfers between devices: 406 us -> none  [head_total(): return lax.psum(values.astype(jnp.bfloat16), 'mp').astype(jnp.float32)]
    pallas_call x0 -> x1, Pallas kernels: none -> 287 us  [per_device(): pl.pallas_call(functools.partial(kernel, n_pipe, n_seq, n_mp), out_shape=...]
    dot_general x75 -> x0, matrix products: 141 us -> none  [the longest x5 22 us: per_device(): jnp.einsum('tc,dc->td', q_grad, query_map, preferred_element_type=jnp.flo...]
    reduce_scatter x5 -> x0, waiting for transfers between devices: 60.2 us -> none  [per_device(): lax.psum_scatter(jnp.concatenate([value_term.reshape(row_count, -1), key_...]
    all_gather x10 -> x0, blocking collectives: 52.2 us -> none  [the longest x5 26.1 us: per_device(): lax.all_gather(value_rows, 'seq', axis=0, tiled=True)]
    ppermute x16 -> x0, starting transfers between devices: 33.8 us -> none  [shifted(): return lax.ppermute(x, axis, pairs)]
    unnamed x34 -> x0, other arithmetic: 30.4 us -> none
    convert_element_type x16 -> x0, other arithmetic: 22.2 us -> none  [the longest x4 11.4 us: per_device(): (grad_dec.astype(jnp.float32) + jnp.where(encoder, 0.0, back_q)).astype(j...]
  transfers between devices with their start and end apart: 30 -> 0, of which waited for: 14 -> 0; matrix products, arithmetic and copies ran while one was open for 11% -> 0% of each run, Pallas kernels for 0% -> 0%
where the time goes in v1:
time: 295 us; the launch traced here: 291 us
  Pallas kernels  287 us (97%)
  local copies, waits for them, and re-layouts  3.54 us (1%)
    pallas_call x1, Pallas kernels, per_device(): pl.pallas_call(functools.partial(kernel, n_pipe, n_seq, n_mp), out_shape=...  287 us

profile of v1, /device:TPU:0, one launch (start us, length us, event | category | flops | bytes accessed | tf_op | source)
XLA Modules:
  0.0 291.3 jit_solution(15933098592803161476)
XLA Ops:
  1.3 286.5 %shard_map.113 = (bf16[1,2,64,1024]{3,2,1,0:T(8,128)(2,1)}, bf16[1,2,2,64,1024]{4,3,2,1,0:T(8,128)(2,1)}) custom-call(bf16[2,64,4096]{2,1,0:T(8,128)(2,1)} %enc_ref.1, bf16[2,64,4096]{2,1,0:T(8,128)(2,1)} %dec_ref.1, s32[2,128]{1,0:T(2,128)} %doc_ref.1, s32[1]{0:T(128)S(6)} %copy.14.count_ref, f32[1,4096]{1,0:T(1,128)} %gain_ref.1, ...), custom_call_target="tpu_custom_call" | custom-call | tf_op jit(solution)/shard_map/pallas_call | solution.py:583
  287.8 1.7 copy.15
  289.5 1.9 copy.16

commit v2 on v1

v2 whole, which is shorter than its diff:
```python
import functools

import jax
import jax.numpy as jnp
from jax import lax
from jax.experimental import pallas as pl
from jax.experimental.pallas import tpu as pltpu
from jax.sharding import PartitionSpec as P

HEADS = 8
HS = 256
PAD = 128

epsilon = 1e-06
MESH = pl.DeviceIdType.MESH
F32 = jnp.float32
BF16 = jnp.bfloat16


def dot_nn(a, b):
    return jnp.dot(a, b, preferred_element_type=F32)


def dot_nt(a, b):
    return lax.dot_general(a, b, (((1,), (1,)), ((), ())), preferred_element_type=F32)


def dot_tn(a, b):
    return lax.dot_general(a, b, (((0,), (0,)), ((), ())), preferred_element_type=F32)


def kernel(
    n_pipe,
    n_seq,
    n_mp,
    enc_ref,
    dec_ref,
    doc_ref,
    count_ref,
    gain_ref,
    wq_hbm,
    wk_hbm,
    wv_hbm,
    wo_hbm,
    og_ref,
    so_ref,
    sg_ref,
    wq,
    wk,
    wv,
    wo,
    w_sem,
    mask,
    upd_recv,
    enc_recv,
    enc_cur,
    src_cur,
    q_acc,
    k_acc,
    v_acc,
    queries,
    q_factor,
    m_factor,
    q_head,
    k_head,
    kv_all,
    portion,
    attended,
    fs_send,
    fs_recv,
    upd_send,
    u_recv,
    d_att,
    kvg_send,
    kvg_recv,
    q_grad,
    k_grad,
    v_grad,
    dq_buf,
    a_send,
    a_recv,
    b_send,
    b_recv,
    s_send,
    s_recv,
    s_total,
    ahop,
    bhop,
    gb_recv,
    upd_ssem,
    upd_rsem,
    enc_ssem,
    enc_rsem,
    kv_ssem,
    kv_rsem,
    fs_ssem,
    fs_rsem,
    u_ssem,
    u_rsem,
    kvg_ssem,
    kvg_rsem,
    a_ssem,
    a_rsem,
    b_ssem,
    b_rsem,
    s_ssem,
    s_rsem,
    gb_ssem,
    gb_rsem,
):
    pipe = lax.axis_index("pipe")
    seq = lax.axis_index("seq")
    z = lax.axis_index("mp")
    batches, toks, width = enc_ref.shape
    share = width // n_mp
    heads = HEADS // n_mp
    units = heads * HS
    scale = HS ** (-0.5)
    last = n_pipe - 1

    def at_mp(j):
        return (pipe, seq, j)

    def at_seq(i):
        return (pipe, i, z)

    def copy(src, dst, ssem, rsem, device):
        return pltpu.make_async_remote_copy(
            src_ref=src,
            dst_ref=dst,
            send_sem=ssem,
            recv_sem=rsem,
            device_id=device,
            device_id_type=MESH,
        )

    weight_loads = [
        pltpu.make_async_copy(hbm.at[0], vmem, w_sem.at[i])
        for i, (hbm, vmem) in enumerate(
            [(wk_hbm, wk), (wv_hbm, wv), (wq_hbm, wq), (wo_hbm, wo)]
        )
    ]
    for load in weight_loads:
        load.start()

    barrier = pltpu.get_barrier_semaphore()
    for k in range(1, n_mp):
        pl.semaphore_signal(
            barrier, inc=1, device_id=at_mp(lax.rem(z + k, n_mp)), device_id_type=MESH
        )
    for k in range(1, n_seq):
        pl.semaphore_signal(
            barrier, inc=1, device_id=at_seq(lax.rem(seq + k, n_seq)), device_id_type=MESH
        )

    @pl.when(pipe > 0)
    def _():
        for j in range(n_mp):
            pl.semaphore_signal(
                barrier, inc=1, device_id=(pipe - 1, seq, j), device_id_type=MESH
            )

    @pl.when(pipe < last)
    def _():
        for j in range(n_mp):
            pl.semaphore_signal(
                barrier, inc=1, device_id=(pipe + 1, seq, j), device_id_type=MESH
            )

    edge = jnp.where(pipe > 0, n_mp, 0) + jnp.where(pipe < last, n_mp, 0)
    pl.semaphore_wait(barrier, n_mp - 1 + n_seq - 1 + edge)

    encoder = pipe < count_ref[0]
    prev_encoder = pipe - 1 < count_ref[0]

    def cut(ref, m, j):
        return ref[m, :, pl.ds(pl.multiple_of(j * share, share), share)]

    def gain_of(j):
        return gain_ref[:, pl.ds(pl.multiple_of(j * share, share), share)]

    def chunk_rows(ref, j):
        return ref[pl.ds(pl.multiple_of(j * share, share), share), :]

    def chunk_cols(ref, j):
        return ref[:, pl.ds(pl.multiple_of(j * share, share), share)]

    length = n_seq * toks
    for m in range(batches):
        row = doc_ref[m : m + 1, :].astype(F32)
        spread = jnp.broadcast_to(row, (length, length))
        mask[m] = (spread == spread.T).astype(F32)
    eye = (
        lax.broadcasted_iota(jnp.int32, (toks, PAD), 0)
        == lax.broadcasted_iota(jnp.int32, (toks, PAD), 1)
    ).astype(F32)
    my_rows = pl.ds(pl.multiple_of(seq * toks, toks), toks)
    none = jnp.zeros((toks, 1), F32)

    def keys_of(m, h):
        return kv_all[m, :, :, h * HS : (h + 1) * HS].reshape(length, HS)

    def values_of(m, h):
        return kv_all[m, :, :, units + h * HS : units + (h + 1) * HS].reshape(length, HS)

    def enc_copy(m, device):
        return copy(enc_cur.at[m], enc_recv.at[m], enc_ssem.at[m], enc_rsem.at[m], device)

    def kv_copy(m, slot, peer, owner):
        return copy(
            kv_all.at[m, seq], kv_all.at[m, owner], kv_ssem.at[m, slot], kv_rsem.at[m, owner],
            at_seq(peer),
        )

    def kvg_copy(m, slot, peer, owner):
        return copy(
            kvg_send.at[m, peer], kvg_recv.at[m, owner], kvg_ssem.at[m, slot],
            kvg_rsem.at[m, owner], at_seq(peer),
        )

    def fs_copy(m, j, owner):
        return copy(
            fs_send.at[m, j], fs_recv.at[m, owner], fs_ssem.at[m, j], fs_rsem.at[m, owner],
            at_mp(j),
        )

    def upd_copy(m, j, owner, device):
        return copy(
            upd_send.at[m], upd_recv.at[m, owner], upd_ssem.at[m, j], upd_rsem.at[m, owner],
            device,
        )

    def u_copy(m, j, owner, device):
        return copy(
            ahop.at[m], u_recv.at[m, owner], u_ssem.at[m, j], u_rsem.at[m, owner], device
        )

    def stat_copy(m, j, owner):
        return copy(
            s_send.at[m], s_recv.at[m, owner], s_ssem.at[m, j], s_rsem.at[m, owner], at_mp(j)
        )

    def a_copy(m, j, owner):
        return copy(
            a_send.at[m, j], a_recv.at[m, owner], a_ssem.at[m, j], a_rsem.at[m, owner], at_mp(j)
        )

    def b_copy(m, j, owner):
        return copy(
            b_send.at[m, j], b_recv.at[m, owner], b_ssem.at[m, j], b_rsem.at[m, owner], at_mp(j)
        )

    def gb_copy(m, device):
        return copy(bhop.at[m], gb_recv.at[m], gb_ssem.at[m], gb_rsem.at[m], device)

    def forward_a(m):
        @pl.when(pipe == 0)
        def _():
            def fill(j, carry):
                upd_recv[m, j] = cut(enc_ref, m, j)
                return carry

            lax.fori_loop(0, n_mp, fill, 0)

        @pl.when(pipe > 0)
        def _():
            enc_copy(m, at_mp(z)).wait_recv()

        k_acc[m] = jnp.zeros((toks, units), F32)
        v_acc[m] = jnp.zeros((toks, units), F32)
        q_acc[m] = jnp.zeros((toks, units), F32)

        def project(k, sums):
            j = lax.rem(z + k, n_mp)

            @pl.when(pipe > 0)
            def _():
                upd_copy(m, j, j, at_mp(z)).wait_recv()

            fresh = upd_recv[m, j].astype(F32)
            enc = jnp.where(prev_encoder, fresh, enc_recv[m, j].astype(F32))
            dec = jnp.where(prev_encoder, cut(dec_ref, m, j).astype(F32), fresh)
            src = jnp.where(encoder, enc, dec)
            enc_cur[m, j] = enc.astype(BF16)
            src_cur[m, j] = src.astype(BF16)
            m_part = (enc * gain_of(j)).astype(BF16)
            k_acc[m] += dot_nn(m_part, chunk_rows(wk, j))
            v_acc[m] += dot_nn(m_part, chunk_rows(wv, j))
            return (
                sums[0] + jnp.sum(src * src, axis=-1, keepdims=True),
                sums[1] + jnp.sum(enc * enc, axis=-1, keepdims=True),
            )

        q_square, m_square = lax.fori_loop(0, n_mp, project, (none, none))
        q_factor[m] = lax.rsqrt(q_square / width + epsilon)
        m_factor[m] = lax.rsqrt(m_square / width + epsilon)

        for h in range(heads):
            lanes = slice(h * HS, (h + 1) * HS)
            keys = k_acc[m, :, lanes] * m_factor[m]
            head = lax.rsqrt(jnp.mean(keys * keys, axis=-1, keepdims=True) + epsilon)
            k_head[m, h] = head
            kv_all[m, seq, :, lanes] = (keys * head).astype(BF16)
        kv_all[m, seq, :, units:] = (v_acc[m] * m_factor[m]).astype(BF16)
        for k in range(1, n_seq):
            kv_copy(m, k, lax.rem(seq + k, n_seq), seq).start()

        @pl.when(pipe < last)
        def _():
            enc_copy(m, (pipe + 1, seq, z)).start()

        if m == 0:
            weight_loads[2].wait()

        def project_q(j, carry):
            q_part = (src_cur[m, j].astype(F32) * gain_of(j)).astype(BF16)
            q_acc[m] += dot_nn(q_part, chunk_rows(wq, j))
            return carry

        lax.fori_loop(0, n_mp, project_q, 0)
        for h in range(heads):
            lanes = slice(h * HS, (h + 1) * HS)
            found = q_acc[m, :, lanes] * q_factor[m]
            head = lax.rsqrt(jnp.mean(found * found, axis=-1, keepdims=True) + epsilon)
            q_head[m, h] = head
            queries[m, :, lanes] = (found * head).astype(BF16)

    def forward_b(m):
        for k in range(1, n_seq):
            peer = lax.rem(seq + k, n_seq)
            kv_copy(m, k, peer, peer).wait_recv()
        same = mask[m, my_rows, :]
        for h in range(heads):
            lanes = slice(h * HS, (h + 1) * HS)
            scores = dot_nt(queries[m, :, lanes], keys_of(m, h)) * scale
            weights = jnp.exp(scores) * same
            totals = jnp.sum(weights, axis=-1, keepdims=True)
            summed = dot_nn(weights.astype(BF16), values_of(m, h))
            attended[m, :, lanes] = (summed / totals).astype(BF16)
            portion[m, h] = weights / totals

        if m == 0:
            weight_loads[3].wait()

        def emit(k, carry):
            j = lax.rem(z + 1 + k, n_mp)
            fs_send[m, j] = dot_nn(attended[m], chunk_cols(wo, j)).astype(BF16)

            @pl.when(k < n_mp - 1)
            def _():
                fs_copy(m, j, z).start()

            return carry

        lax.fori_loop(0, n_mp, emit, 0)

    def forward_c(m):
        branch = fs_send[m, z].astype(F32)
        for k in range(1, n_mp):
            j = lax.rem(z + k, n_mp)
            fs_copy(m, j, j).wait_recv()
            branch = branch + fs_recv[m, j].astype(F32)
        updated = (src_cur[m, z].astype(F32) + branch).astype(BF16)
        upd_send[m] = updated

        @pl.when(pipe < last)
        def _():
            for j in range(n_mp):
                upd_copy(m, j, z, (pipe + 1, seq, j)).start()

        so_ref[0, m] = updated

    for load in weight_loads[:2]:
        load.wait()
    forward_a(0)
    forward_b(0)
    for m in range(1, batches):
        forward_a(m)
        forward_c(m - 1)
        forward_b(m)
    forward_c(batches - 1)

    def sort_a(dq, dm):
        return jnp.where(encoder, dq + dm, jnp.where(prev_encoder, dm, dq))

    def sort_b(dq, dm):
        return jnp.where(encoder, 0.0, jnp.where(prev_encoder, dq, dm))

    def to_row(column):
        return jnp.sum(column * eye, axis=0, keepdims=True)

    def to_column(row):
        return jnp.sum(row * eye, axis=1, keepdims=True)

    turns = jnp.logical_and(jnp.logical_not(encoder), prev_encoder)
    first = jnp.logical_or(encoder, prev_encoder)

    def backward_a(m):
        @pl.when(pipe == last)
        def _():
            def fill(j, carry):
                start = cut(og_ref, m, j).astype(F32)
                u_recv[m, j] = jnp.where(encoder, 0.0, start).astype(BF16)
                return carry

            lax.fori_loop(0, n_mp, fill, 0)
            start = cut(og_ref, m, z).astype(F32)
            gb_recv[m] = jnp.where(encoder, start, 0.0).astype(BF16)

        def pull(k, total):
            j = lax.rem(z + k, n_mp)

            @pl.when(pipe < last)
            def _():
                u_copy(m, j, j, at_mp(z)).wait_recv()

            return total + dot_nt(u_recv[m, j], chunk_cols(wo, j))

        d_att[m] = lax.fori_loop(0, n_mp, pull, jnp.zeros((toks, units), F32)).astype(BF16)

        for h in range(heads):
            lanes = slice(h * HS, (h + 1) * HS)
            wide = slice(units + h * HS, units + (h + 1) * HS)
            probs = portion[m, h]
            pulled = d_att[m, :, lanes]
            along = dot_nt(pulled, values_of(m, h))
            delta = jnp.sum(
                pulled.astype(F32) * attended[m, :, lanes].astype(F32), axis=-1, keepdims=True
            )
            d_scores = (probs * (along - delta)).astype(BF16)
            asked = queries[m, :, lanes]
            value_term = dot_tn(probs.astype(BF16), pulled)
            key_term = dot_tn(d_scores, asked) * scale
            kvg_send[m, :, :, lanes] = key_term.astype(BF16).reshape(n_seq, toks, HS)
            kvg_send[m, :, :, wide] = value_term.astype(BF16).reshape(n_seq, toks, HS)
            d_queries = dot_nn(d_scores, keys_of(m, h)) * scale
            normed = asked.astype(F32)
            mean = jnp.mean(d_queries * normed, axis=-1, keepdims=True)
            q_grad[m, :, lanes] = (q_head[m, h] * (d_queries - normed * mean)).astype(BF16)

        for k in range(1, n_seq):
            kvg_copy(m, k, lax.rem(seq + k, n_seq), seq).start()

        def ask(j, carry):
            dq_buf[m, j] = dot_nt(q_grad[m], chunk_rows(wq, j))
            return carry

        lax.fori_loop(0, n_mp, ask, 0)

    def backward_b(m):
        q_stat = jnp.sum(q_grad[m].astype(F32) * q_acc[m], axis=-1, keepdims=True)
        d_kv = kvg_send[m, seq].astype(F32)
        for k in range(1, n_seq):
            peer = lax.rem(seq + k, n_seq)
            kvg_copy(m, k, peer, peer).wait_recv()
            d_kv = d_kv + kvg_recv[m, peer].astype(F32)
        v_grad[m] = d_kv[:, units:].astype(BF16)
        for h in range(heads):
            lanes = slice(h * HS, (h + 1) * HS)
            d_keys = d_kv[:, lanes]
            normed = kv_all[m, seq, :, lanes].astype(F32)
            mean = jnp.mean(d_keys * normed, axis=-1, keepdims=True)
            k_grad[m, :, lanes] = (k_head[m, h] * (d_keys - normed * mean)).astype(BF16)
        m_stat = jnp.sum(
            k_grad[m].astype(F32) * k_acc[m] + v_grad[m].astype(F32) * v_acc[m],
            axis=-1,
            keepdims=True,
        )
        s_send[m, 0:1, :] = to_row(sort_a(q_stat, m_stat))
        s_send[m, 1:2, :] = to_row(sort_b(q_stat, m_stat))
        s_send[m, 2:, :] = jnp.zeros((6, PAD), F32)
        for k in range(1, n_mp):
            stat_copy(m, lax.rem(z + k, n_mp), z).start()

        def spread_out(k, carry):
            j = lax.rem(z + 1 + k, n_mp)
            dm = dot_nt(k_grad[m], chunk_rows(wk, j)) + dot_nt(v_grad[m], chunk_rows(wv, j))
            dq = dq_buf[m, j]
            a_send[m, j] = sort_a(dq, dm).astype(BF16)

            @pl.when(k < n_mp - 1)
            def _():
                a_copy(m, j, z).start()

            b_send[m, j] = sort_b(dq, dm).astype(BF16)
            return carry

        lax.fori_loop(0, n_mp, spread_out, 0)

    def norm_back(values, factor, total, stat):
        return factor * (gain_of(z) * total - values * (factor * factor * (stat / width)))

    def backward_c(m):
        stats = s_send[m]
        for k in range(1, n_mp):
            j = lax.rem(z + k, n_mp)
            stat_copy(m, j, j).wait_recv()
            stats = stats + s_recv[m, j]
        s_total[m] = stats
        total = a_send[m, z].astype(F32)
        for k in range(1, n_mp):
            j = lax.rem(z + k, n_mp)
            a_copy(m, j, j).wait_recv()
            total = total + a_recv[m, j].astype(F32)

        @pl.when(pipe < last)
        def _():
            gb_copy(m, at_mp(z)).wait_recv()

        base = jnp.where(turns, gb_recv[m].astype(F32), u_recv[m, z].astype(F32))
        values = jnp.where(turns, enc_cur[m, z].astype(F32), src_cur[m, z].astype(F32))
        factor = jnp.where(turns, m_factor[m], q_factor[m])
        fresh = base + norm_back(values, factor, total, to_column(stats[0:1, :]))
        ahop[m] = fresh.astype(BF16)

        @pl.when(pipe > 0)
        def _():
            for j in range(n_mp):
                u_copy(m, j, z, (pipe - 1, seq, j)).start()

    def finish(m, b_new):
        a_new = ahop[m].astype(F32)
        sg_ref[0, 0, m] = jnp.where(first, a_new, b_new).astype(BF16)
        sg_ref[0, 1, m] = jnp.where(first, b_new, a_new).astype(BF16)

    def backward_d(m):
        @pl.when(pipe == 0)
        def _():
            finish(m, gb_recv[m].astype(F32))

        @pl.when(pipe > 0)
        def _():
            total = b_send[m, z].astype(F32)
            for k in range(1, n_mp):
                j = lax.rem(z + k, n_mp)
                b_copy(m, j, j).wait_recv()
                total = total + b_recv[m, j].astype(F32)
            base = jnp.where(turns, u_recv[m, z].astype(F32), gb_recv[m].astype(F32))
            values = jnp.where(turns, src_cur[m, z].astype(F32), enc_cur[m, z].astype(F32))
            factor = jnp.where(turns, q_factor[m], m_factor[m])
            fresh = base + norm_back(values, factor, total, to_column(s_total[m, 1:2, :]))
            bhop[m] = fresh.astype(BF16)
            gb_copy(m, (pipe - 1, seq, z)).start()
            finish(m, fresh)

    backward_a(0)
    backward_b(0)
    for m in range(1, batches):
        backward_a(m)
        backward_c(m - 1)
        backward_b(m)
    backward_c(batches - 1)

    @pl.when(pipe > 0)
    def _():
        for m in range(batches):
            for j in range(n_mp):
                u_copy(m, j, z, (pipe - 1, seq, j)).wait_send()
            for k in range(1, n_mp):
                b_copy(m, lax.rem(z + k, n_mp), z).start()

    for m in range(batches):
        backward_d(m)

    for m in range(batches):
        for k in range(1, n_seq):
            peer = lax.rem(seq + k, n_seq)
            kv_copy(m, k, peer, seq).wait_send()
            kvg_copy(m, k, peer, seq).wait_send()
        for k in range(1, n_mp):
            j = lax.rem(z + k, n_mp)
            fs_copy(m, j, z).wait_send()
            stat_copy(m, j, z).wait_send()
            a_copy(m, j, z).wait_send()

    @pl.when(pipe < last)
    def _():
        for m in range(batches):
            enc_copy(m, (pipe + 1, seq, z)).wait_send()
            for j in range(n_mp):
                upd_copy(m, j, z, (pipe + 1, seq, j)).wait_send()

    @pl.when(pipe > 0)
    def _():
        for m in range(batches):
            gb_copy(m, (pipe - 1, seq, z)).wait_send()
            for k in range(1, n_mp):
                b_copy(m, lax.rem(z + k, n_mp), z).wait_send()


def per_device(n_pipe, n_seq, n_mp, enc_in, dec_in, doc_ids, enc_sections, norm_gain,
               q_weight, k_weight, v_weight, o_weight, out_grad):
    batches, toks, width = enc_in.shape
    share = width // n_mp
    heads = HEADS // n_mp
    units = heads * HS
    length = n_seq * toks
    vmem = pl.BlockSpec(memory_space=pltpu.VMEM)
    hbm = pl.BlockSpec(memory_space=pl.ANY)
    smem = pl.BlockSpec(memory_space=pltpu.SMEM)
    V = pltpu.VMEM
    dma = pltpu.SemaphoreType.DMA
    scratch = [
        V((width, units), BF16),
        V((width, units), BF16),
        V((width, units), BF16),
        V((units, width), BF16),
        dma((4,)),
        V((batches, length, length), F32),
        V((batches, n_mp, toks, share), BF16),
        V((batches, n_mp, toks, share), BF16),
        V((batches, n_mp, toks, share), BF16),
        V((batches, n_mp, toks, share), BF16),
        V((batches, toks, units), F32),
        V((batches, toks, units), F32),
        V((batches, toks, units), F32),
        V((batches, toks, units), BF16),
        V((batches, toks, 1), F32),
        V((batches, toks, 1), F32),
        V((batches, heads, toks, 1), F32),
        V((batches, heads, toks, 1), F32),
        V((batches, n_seq, toks, 2 * units), BF16),
        V((batches, heads, toks, length), F32),
        V((batches, toks, units), BF16),
        V((batches, n_mp, toks, share), BF16),
        V((batches, n_mp, toks, share), BF16),
        V((batches, toks, share), BF16),
        V((batches, n_mp, toks, share), BF16),
        V((batches, toks, units), BF16),
        V((batches, n_seq, toks, 2 * units), BF16),
        V((batches, n_seq, toks, 2 * units), BF16),
        V((batches, toks, units), BF16),
        V((batches, toks, units), BF16),
        V((batches, toks, units), BF16),
        V((batches, n_mp, toks, share), F32),
        V((batches, n_mp, toks, share), BF16),
        V((batches, n_mp, toks, share), BF16),
        V((batches, n_mp, toks, share), BF16),
        V((batches, n_mp, toks, share), BF16),
        V((batches, 8, PAD), F32),
        V((batches, n_mp, 8, PAD), F32),
        V((batches, 8, PAD), F32),
        V((batches, toks, share), BF16),
        V((batches, toks, share), BF16),
        V((batches, toks, share), BF16),
        dma((batches, n_mp)),
        dma((batches, n_mp)),
        dma((batches,)),
        dma((batches,)),
        dma((batches, n_seq)),
        dma((batches, n_seq)),
        dma((batches, n_mp)),
        dma((batches, n_mp)),
        dma((batches, n_mp)),
        dma((batches, n_mp)),
        dma((batches, n_seq)),
        dma((batches, n_seq)),
        dma((batches, n_mp)),
        dma((batches, n_mp)),
        dma((batches, n_mp)),
        dma((batches, n_mp)),
        dma((batches, n_mp)),
        dma((batches, n_mp)),
        dma((batches,)),
        dma((batches,)),
    ]
    return pl.pallas_call(
        functools.partial(kernel, n_pipe, n_seq, n_mp),
        out_shape=(
            jax.ShapeDtypeStruct((1, batches, toks, share), BF16),
            jax.ShapeDtypeStruct((1, 2, batches, toks, share), BF16),
        ),
        in_specs=[vmem, vmem, vmem, smem, vmem, hbm, hbm, hbm, hbm, vmem],
        out_specs=(vmem, vmem),
        scratch_shapes=scratch,
        compiler_params=pltpu.CompilerParams(
            collective_id=0, has_side_effects=True, vmem_limit_bytes=56 * 1024 * 1024
        ),
    )(enc_in, dec_in, doc_ids, enc_sections, norm_gain, q_weight, k_weight, v_weight, o_weight,
      out_grad)


def solution(mesh):
    sizes = (mesh.shape["pipe"], mesh.shape["seq"], mesh.shape["mp"])
    return jax.shard_map(
        functools.partial(per_device, *sizes),
        mesh=mesh,
        in_specs=(
            P(None, "seq", None),
            P(None, "seq", None),
            P(),
            P(),
            P("pipe", None),
            P("pipe", None, "mp"),
            P("pipe", None, "mp"),
            P("pipe", None, "mp"),
            P("pipe", "mp", None),
            P(None, "seq", None),
        ),
        out_specs=(P("pipe", None, "seq", "mp"), P("pipe", None, None, "seq", "mp")),
        check_vma=False,
    )
```

time: 295 us -> 252 us (0.85); the launches traced: 291 us -> 252 us
  Pallas kernels: 287 us -> 247 us
    pallas_call x1, Pallas kernels: 287 us -> 247 us  [per_device(): pl.pallas_call(functools.partial(kernel, n_pipe, n_seq, n_mp), out_shape=...]
where the time goes in v2:
time: 252 us
  Pallas kernels  247 us (98%)
  local copies, waits for them, and re-layouts  3.54 us (1%)
    pallas_call x1, Pallas kernels, per_device(): pl.pallas_call(functools.partial(kernel, n_pipe, n_seq, n_mp), out_shape=...  247 us

profile of v2, /device:TPU:0, one launch (start us, length us, event | category | flops | bytes accessed | tf_op | source)
XLA Modules:
  0.0 251.8 jit_solution(7305239671528236406)
XLA Ops:
  1.3 246.9 %shard_map.113 = (bf16[1,2,64,1024]{3,2,1,0:T(8,128)(2,1)}, bf16[1,2,2,64,1024]{4,3,2,1,0:T(8,128)(2,1)}) custom-call(bf16[2,64,4096]{2,1,0:T(8,128)(2,1)} %enc_ref.1, bf16[2,64,4096]{2,1,0:T(8,128)(2,1)} %dec_ref.1, s32[2,128]{1,0:T(2,128)} %doc_ref.1, s32[1]{0:T(128)S(6)} %copy.14.count_ref, f32[1,4096]{1,0:T(1,128)} %gain_ref.1, ...), custom_call_target="tpu_custom_call" | custom-call | tf_op jit(solution)/shard_map/pallas_call | solution.py:667
  248.2 1.7 copy.15
  249.9 1.9 copy.16

commit v3 on v2

--- a/solution.py
+++ b/solution.py
@@ -84,6 +84,9 @@
     s_send,
     s_recv,
     s_total,
+    fs_relay,
+    a_relay,
+    b_relay,
     ahop,
     bhop,
     gb_recv,
@@ -105,6 +108,9 @@
     b_rsem,
     s_ssem,
     s_rsem,
+    relay_ssem,
+    relay_rsem,
+    pass_ssem,
     gb_ssem,
     gb_rsem,
 ):
@@ -253,6 +259,99 @@
     def gb_copy(m, device):
         return copy(bhop.at[m], gb_recv.at[m], gb_ssem.at[m], gb_rsem.at[m], device)
 
+    chain = n_mp == 4
+    far = n_mp - 1 - z
+    upper = z >= n_mp // 2
+    near_z = jnp.where(upper, far, z)
+    is_end = near_z == 0 if chain else z < 0
+    is_mid = near_z == 1 if chain else z < 0
+    partner = jnp.where(upper, n_mp - 2, 1)
+    other_end = jnp.where(upper, 0, n_mp - 1)
+    this_end = jnp.where(upper, n_mp - 1, 0)
+
+    def mirror(j):
+        return jnp.where(upper, n_mp - 1 - j, j)
+
+    def reduce_order(k):
+        if not chain:
+            return lax.rem(z + 1 + k, n_mp)
+        mid = jnp.where(k == 0, 2, jnp.where(k == 3, 3, k - 1))
+        return mirror(jnp.where(is_end, 3 - k, mid))
+
+    def gather_order(k):
+        if not chain:
+            return lax.rem(z + k, n_mp)
+        mid = jnp.where(k == 0, 1, jnp.where(k == 1, 3, jnp.where(k == 2, 0, 2)))
+        return mirror(jnp.where(is_end, k, mid))
+
+    def skipped(j):
+        return jnp.logical_and(is_end, j == far)
+
+    def kept(j):
+        return jnp.logical_not(skipped(j))
+
+    def relay_copy(which, m, send, relay):
+        return copy(
+            send.at[m, far], relay.at[m], relay_ssem.at[which, m], relay_rsem.at[which, m],
+            at_mp(partner),
+        )
+
+    def pass_copy(which, m, buffer, rsem):
+        return copy(
+            buffer.at[m, other_end], buffer.at[m, other_end], pass_ssem.at[which, m],
+            rsem.at[m, other_end], at_mp(this_end),
+        )
+
+    def reduce_part(which, m, k, j, block, send, relay, direct):
+        send[m, j] = block.astype(BF16)
+        closing = jnp.logical_and(is_mid, k == n_mp - 1)
+        opening = jnp.logical_and(is_end, k == 0)
+
+        @pl.when(closing)
+        def _():
+            relay_copy(which, m, send, relay).wait_recv()
+            send[m, j] = (block + relay[m].astype(F32)).astype(BF16)
+
+        @pl.when(opening)
+        def _():
+            relay_copy(which, m, send, relay).start()
+
+        @pl.when(jnp.logical_and(j != z, kept(j)))
+        def _():
+            direct(m, j, z).start()
+
+    def reduced(m, send, recv, direct):
+        total = send[m, z].astype(F32)
+        for k in range(1, n_mp):
+            j = lax.rem(z + k, n_mp)
+
+            @pl.when(kept(j))
+            def _():
+                direct(m, j, j).wait_recv()
+
+            total = total + recv[m, j].astype(F32)
+        return total
+
+    def reduce_drain(which, m, send, relay, direct):
+        for k in range(1, n_mp):
+            j = lax.rem(z + k, n_mp)
+
+            @pl.when(kept(j))
+            def _():
+                direct(m, j, z).wait_send()
+
+        @pl.when(is_end)
+        def _():
+            relay_copy(which, m, send, relay).wait_send()
+
+    @pl.when(is_end)
+    def _():
+        for m in range(batches):
+            for recv in (fs_recv, a_recv, b_recv):
+                recv[m, far] = jnp.zeros((toks, share), BF16)
+
+    hop_order = [lax.rem(z + k, n_mp) for k in sorted(range(n_mp), key=lambda k: (k == 0, k != 2))]
+
     def forward_a(m):
         @pl.when(pipe == 0)
         def _():
@@ -271,11 +370,15 @@
         q_acc[m] = jnp.zeros((toks, units), F32)
 
         def project(k, sums):
-            j = lax.rem(z + k, n_mp)
+            j = gather_order(k)
 
             @pl.when(pipe > 0)
             def _():
                 upd_copy(m, j, j, at_mp(z)).wait_recv()
+
+                @pl.when(jnp.logical_and(is_mid, k == 1))
+                def _():
+                    pass_copy(0, m, upd_recv, upd_rsem).start()
 
             fresh = upd_recv[m, j].astype(F32)
             enc = jnp.where(prev_encoder, fresh, enc_recv[m, j].astype(F32))
@@ -343,30 +446,25 @@
             weight_loads[3].wait()
 
         def emit(k, carry):
-            j = lax.rem(z + 1 + k, n_mp)
-            fs_send[m, j] = dot_nn(attended[m], chunk_cols(wo, j)).astype(BF16)
-
-            @pl.when(k < n_mp - 1)
-            def _():
-                fs_copy(m, j, z).start()
-
+            j = reduce_order(k)
+            block = dot_nn(attended[m], chunk_cols(wo, j))
+            reduce_part(0, m, k, j, block, fs_send, fs_relay, fs_copy)
             return carry
 
         lax.fori_loop(0, n_mp, emit, 0)
 
     def forward_c(m):
-        branch = fs_send[m, z].astype(F32)
-        for k in range(1, n_mp):
-            j = lax.rem(z + k, n_mp)
-            fs_copy(m, j, j).wait_recv()
-            branch = branch + fs_recv[m, j].astype(F32)
+        branch = reduced(m, fs_send, fs_recv, fs_copy)
         updated = (src_cur[m, z].astype(F32) + branch).astype(BF16)
         upd_send[m] = updated
 
         @pl.when(pipe < last)
         def _():
-            for j in range(n_mp):
-                upd_copy(m, j, z, (pipe + 1, seq, j)).start()
+            for j in hop_order:
+
+                @pl.when(kept(j))
+                def _():
+                    upd_copy(m, j, z, (pipe + 1, seq, j)).start()
 
         so_ref[0, m] = updated
 
@@ -408,11 +506,15 @@
             gb_recv[m] = jnp.where(encoder, start, 0.0).astype(BF16)
 
         def pull(k, total):
-            j = lax.rem(z + k, n_mp)
+            j = gather_order(k)
 
             @pl.when(pipe < last)
             def _():
                 u_copy(m, j, j, at_mp(z)).wait_recv()
+
+                @pl.when(jnp.logical_and(is_mid, k == 1))
+                def _():
+                    pass_copy(1, m, u_recv, u_rsem).start()
 
             return total + dot_nt(u_recv[m, j], chunk_cols(wo, j))
 
@@ -473,15 +575,10 @@
             stat_copy(m, lax.rem(z + k, n_mp), z).start()
 
         def spread_out(k, carry):
-            j = lax.rem(z + 1 + k, n_mp)
+            j = reduce_order(k)
             dm = dot_nt(k_grad[m], chunk_rows(wk, j)) + dot_nt(v_grad[m], chunk_rows(wv, j))
             dq = dq_buf[m, j]
-            a_send[m, j] = sort_a(dq, dm).astype(BF16)
-
-            @pl.when(k < n_mp - 1)
-            def _():
-                a_copy(m, j, z).start()
-
+            reduce_part(1, m, k, j, sort_a(dq, dm), a_send, a_relay, a_copy)
             b_send[m, j] = sort_b(dq, dm).astype(BF16)
             return carry
 
@@ -497,11 +594,7 @@
             stat_copy(m, j, j).wait_recv()
             stats = stats + s_recv[m, j]
         s_total[m] = stats
-        total = a_send[m, z].astype(F32)
-        for k in range(1, n_mp):
-            j = lax.rem(z + k, n_mp)
-            a_copy(m, j, j).wait_recv()
-            total = total + a_recv[m, j].astype(F32)
+        total = reduced(m, a_send, a_recv, a_copy)
 
         @pl.when(pipe < last)
         def _():
@@ -515,8 +608,11 @@
 
         @pl.when(pipe > 0)
         def _():
-            for j in range(n_mp):
-                u_copy(m, j, z, (pipe - 1, seq, j)).start()
+            for j in hop_order:
+
+                @pl.when(kept(j))
+                def _():
+                    u_copy(m, j, z, (pipe - 1, seq, j)).start()
 
     def finish(m, b_new):
         a_new = ahop[m].astype(F32)
@@ -530,11 +626,7 @@
 
         @pl.when(pipe > 0)
         def _():
-            total = b_send[m, z].astype(F32)
-            for k in range(1, n_mp):
-                j = lax.rem(z + k, n_mp)
-                b_copy(m, j, j).wait_recv()
-                total = total + b_recv[m, j].astype(F32)
+            total = reduced(m, b_send, b_recv, b_copy)
             base = jnp.where(turns, u_recv[m, z].astype(F32), gb_recv[m].astype(F32))
             values = jnp.where(turns, src_cur[m, z].astype(F32), enc_cur[m, z].astype(F32))
             factor = jnp.where(turns, q_factor[m], m_factor[m])
@@ -554,10 +646,31 @@
     @pl.when(pipe > 0)
     def _():
         for m in range(batches):
-            for j in range(n_mp):
-                u_copy(m, j, z, (pipe - 1, seq, j)).wait_send()
+            for j in hop_order:
+
+                @pl.when(kept(j))
+                def _():
+                    u_copy(m, j, z, (pipe - 1, seq, j)).wait_send()
+
+            @pl.when(is_end)
+            def _():
+                relay_copy(2, m, b_send, b_relay).start()
+
             for k in range(1, n_mp):
-                b_copy(m, lax.rem(z + k, n_mp), z).start()
+                j = lax.rem(z + k, n_mp)
+                held = jnp.logical_and(is_mid, j == other_end)
+
+                @pl.when(jnp.logical_and(kept(j), jnp.logical_not(held)))
+                def _():
+                    b_copy(m, j, z).start()
+
+        @pl.when(is_mid)
+        def _():
+            for m in range(batches):
+                relay_copy(2, m, b_send, b_relay).wait_recv()
+                joined = b_send[m, other_end].astype(F32) + b_relay[m].astype(F32)
+                b_send[m, other_end] = joined.astype(BF16)
+                b_copy(m, other_end, z).start()
 
     for m in range(batches):
         backward_d(m)
@@ -569,23 +682,33 @@
             kvg_copy(m, k, peer, seq).wait_send()
         for k in range(1, n_mp):
             j = lax.rem(z + k, n_mp)
-            fs_copy(m, j, z).wait_send()
             stat_copy(m, j, z).wait_send()
-            a_copy(m, j, z).wait_send()
+        reduce_drain(0, m, fs_send, fs_relay, fs_copy)
+        reduce_drain(1, m, a_send, a_relay, a_copy)
 
     @pl.when(pipe < last)
     def _():
         for m in range(batches):
             enc_copy(m, (pipe + 1, seq, z)).wait_send()
-            for j in range(n_mp):
-                upd_copy(m, j, z, (pipe + 1, seq, j)).wait_send()
+            for j in hop_order:
+
+                @pl.when(kept(j))
+                def _():
+                    upd_copy(m, j, z, (pipe + 1, seq, j)).wait_send()
+
+            @pl.when(is_mid)
+            def _():
+                pass_copy(1, m, u_recv, u_rsem).wait_send()
 
     @pl.when(pipe > 0)
     def _():
         for m in range(batches):
             gb_copy(m, (pipe - 1, seq, z)).wait_send()
-            for k in range(1, n_mp):
-                b_copy(m, lax.rem(z + k, n_mp), z).wait_send()
+            reduce_drain(2, m, b_send, b_relay, b_copy)
+
+            @pl.when(is_mid)
+            def _():
+                pass_copy(0, m, upd_recv, upd_rsem).wait_send()
 
 
 def per_device(n_pipe, n_seq, n_mp, enc_in, dec_in, doc_ids, enc_sections, norm_gain,
@@ -643,6 +766,9 @@
         V((batches, toks, share), BF16),
         V((batches, toks, share), BF16),
         V((batches, toks, share), BF16),
+        V((batches, toks, share), BF16),
+        V((batches, toks, share), BF16),
+        V((batches, toks, share), BF16),
         dma((batches, n_mp)),
         dma((batches, n_mp)),
         dma((batches,)),
@@ -661,6 +787,9 @@
         dma((batches, n_mp)),
         dma((batches, n_mp)),
         dma((batches, n_mp)),
+        dma((3, batches)),
+        dma((3, batches)),
+        dma((2, batches)),
         dma((batches,)),
         dma((batches,)),
     ]

time: 252 us -> 231 us (0.917)
  Pallas kernels: 247 us -> 226 us
    pallas_call x1, Pallas kernels: 247 us -> 226 us  [per_device(): pl.pallas_call(functools.partial(kernel, n_pipe, n_seq, n_mp), out_shape=...]
where the time goes in v3:
time: 231 us
  Pallas kernels  226 us (98%)
  local copies, waits for them, and re-layouts  3.54 us (2%)
    pallas_call x1, Pallas kernels, per_device(): pl.pallas_call(functools.partial(kernel, n_pipe, n_seq, n_mp), out_shape=...  226 us

profile of v3, /device:TPU:0, one launch (start us, length us, event | category | flops | bytes accessed | tf_op | source)
XLA Modules:
  0.0 231.0 jit_solution(740117130876371460)
XLA Ops:
  1.3 226.1 %shard_map.113 = (bf16[1,2,64,1024]{3,2,1,0:T(8,128)(2,1)}, bf16[1,2,2,64,1024]{4,3,2,1,0:T(8,128)(2,1)}) custom-call(bf16[2,64,4096]{2,1,0:T(8,128)(2,1)} %enc_ref.1, bf16[2,64,4096]{2,1,0:T(8,128)(2,1)} %dec_ref.1, s32[2,128]{1,0:T(2,128)} %doc_ref.1, s32[1]{0:T(128)S(6)} %copy.14.count_ref, f32[1,4096]{1,0:T(1,128)} %gain_ref.1, ...), custom_call_target="tpu_custom_call" | custom-call | tf_op jit(solution)/shard_map/pallas_call | solution.py:796
  227.4 1.7 copy.15
  229.1 1.9 copy.16

commit v4 on v3

--- a/solution.py
+++ b/solution.py
@@ -352,7 +352,7 @@
 
     hop_order = [lax.rem(z + k, n_mp) for k in sorted(range(n_mp), key=lambda k: (k == 0, k != 2))]
 
-    def forward_a(m):
+    def forward_a(m, wait_q):
         @pl.when(pipe == 0)
         def _():
             def fill(j, carry):
@@ -361,7 +361,7 @@
 
             lax.fori_loop(0, n_mp, fill, 0)
 
-        @pl.when(pipe > 0)
+        @pl.when(pipe > 1)
         def _():
             enc_copy(m, at_mp(z)).wait_recv()
 
@@ -408,11 +408,11 @@
         for k in range(1, n_seq):
             kv_copy(m, k, lax.rem(seq + k, n_seq), seq).start()
 
-        @pl.when(pipe < last)
+        @pl.when(jnp.logical_and(pipe > 0, pipe < last))
         def _():
             enc_copy(m, (pipe + 1, seq, z)).start()
 
-        if m == 0:
+        if wait_q:
             weight_loads[2].wait()
 
         def project_q(j, carry):
@@ -442,9 +442,7 @@
             attended[m, :, lanes] = (summed / totals).astype(BF16)
             portion[m, h] = weights / totals
 
-        if m == 0:
-            weight_loads[3].wait()
-
+    def forward_out(m):
         def emit(k, carry):
             j = reduce_order(k)
             block = dot_nn(attended[m], chunk_cols(wo, j))
@@ -468,16 +466,6 @@
 
         so_ref[0, m] = updated
 
-    for load in weight_loads[:2]:
-        load.wait()
-    forward_a(0)
-    forward_b(0)
-    for m in range(1, batches):
-        forward_a(m)
-        forward_c(m - 1)
-        forward_b(m)
-    forward_c(batches - 1)
-
     def sort_a(dq, dm):
         return jnp.where(encoder, dq + dm, jnp.where(prev_encoder, dm, dq))
 
@@ -493,7 +481,7 @@
     turns = jnp.logical_and(jnp.logical_not(encoder), prev_encoder)
     first = jnp.logical_or(encoder, prev_encoder)
 
-    def backward_a(m):
+    def backward_pull(m):
         @pl.when(pipe == last)
         def _():
             def fill(j, carry):
@@ -520,6 +508,7 @@
 
         d_att[m] = lax.fori_loop(0, n_mp, pull, jnp.zeros((toks, units), F32)).astype(BF16)
 
+    def backward_a(m):
         for h in range(heads):
             lanes = slice(h * HS, (h + 1) * HS)
             wide = slice(units + h * HS, units + (h + 1) * HS)
@@ -635,45 +624,91 @@
             gb_copy(m, (pipe - 1, seq, z)).start()
             finish(m, fresh)
 
-    backward_a(0)
-    backward_b(0)
-    for m in range(1, batches):
-        backward_a(m)
-        backward_c(m - 1)
-        backward_b(m)
-    backward_c(batches - 1)
-
-    @pl.when(pipe > 0)
+    def backward_rest():
+        @pl.when(pipe > 0)
+        def _():
+            for m in range(batches):
+                for j in hop_order:
+
+                    @pl.when(kept(j))
+                    def _():
+                        u_copy(m, j, z, (pipe - 1, seq, j)).wait_send()
+
+                @pl.when(is_end)
+                def _():
+                    relay_copy(2, m, b_send, b_relay).start()
+
+                for k in range(1, n_mp):
+                    j = lax.rem(z + k, n_mp)
+                    held = jnp.logical_and(is_mid, j == other_end)
+
+                    @pl.when(jnp.logical_and(kept(j), jnp.logical_not(held)))
+                    def _():
+                        b_copy(m, j, z).start()
+
+            @pl.when(is_mid)
+            def _():
+                for m in range(batches):
+                    relay_copy(2, m, b_send, b_relay).wait_recv()
+                    joined = b_send[m, other_end].astype(F32) + b_relay[m].astype(F32)
+                    b_send[m, other_end] = joined.astype(BF16)
+                    b_copy(m, other_end, z).start()
+
+        for m in range(batches):
+            backward_d(m)
+
+    @pl.when(pipe < last)
+    def _():
+        for load in weight_loads[:2]:
+            load.wait()
+        forward_a(0, True)
+        forward_b(0)
+        weight_loads[3].wait()
+        forward_out(0)
+        for m in range(1, batches):
+            forward_a(m, False)
+            forward_c(m - 1)
+            forward_b(m)
+            forward_out(m)
+        forward_c(batches - 1)
+        backward_pull(0)
+        backward_a(0)
+        backward_b(0)
+        for m in range(1, batches):
+            backward_pull(m)
+            backward_a(m)
+            backward_c(m - 1)
+            backward_b(m)
+        backward_c(batches - 1)
+        backward_rest()
+
+    @pl.when(pipe == last)
+    def _():
+        for load in weight_loads:
+            load.wait()
+        for m in range(batches):
+            backward_pull(m)
+        forward_a(0, False)
+        forward_b(0)
+        backward_a(0)
+        backward_b(0)
+        for m in range(1, batches):
+            forward_a(m, False)
+            backward_c(m - 1)
+            forward_b(m)
+            backward_a(m)
+            backward_b(m)
+        backward_c(batches - 1)
+        backward_rest()
+        for m in range(batches):
+            forward_out(m)
+        for m in range(batches):
+            forward_c(m)
+
+    @pl.when(jnp.logical_and(pipe > 0, pipe < last))
     def _():
         for m in range(batches):
-            for j in hop_order:
-
-                @pl.when(kept(j))
-                def _():
-                    u_copy(m, j, z, (pipe - 1, seq, j)).wait_send()
-
-            @pl.when(is_end)
-            def _():
-                relay_copy(2, m, b_send, b_relay).start()
-
-            for k in range(1, n_mp):
-                j = lax.rem(z + k, n_mp)
-                held = jnp.logical_and(is_mid, j == other_end)
-
-                @pl.when(jnp.logical_and(kept(j), jnp.logical_not(held)))
-                def _():
-                    b_copy(m, j, z).start()
-
-        @pl.when(is_mid)
-        def _():
-            for m in range(batches):
-                relay_copy(2, m, b_send, b_relay).wait_recv()
-                joined = b_send[m, other_end].astype(F32) + b_relay[m].astype(F32)
-                b_send[m, other_end] = joined.astype(BF16)
-                b_copy(m, other_end, z).start()
-
-    for m in range(batches):
-        backward_d(m)
+            enc_copy(m, (pipe + 1, seq, z)).wait_send()
 
     for m in range(batches):
         for k in range(1, n_seq):
@@ -689,7 +724,6 @@
     @pl.when(pipe < last)
     def _():
         for m in range(batches):
-            enc_copy(m, (pipe + 1, seq, z)).wait_send()
             for j in hop_order:
 
                 @pl.when(kept(j))

time: 231 us -> 219 us (0.948)
  Pallas kernels: 226 us -> 214 us
    pallas_call x1, Pallas kernels: 226 us -> 214 us  [per_device(): pl.pallas_call(functools.partial(kernel, n_pipe, n_seq, n_mp), out_shape=...]
where the time goes in v4:
time: 219 us
  Pallas kernels  214 us (98%)
  local copies, waits for them, and re-layouts  3.54 us (2%)
    pallas_call x1, Pallas kernels, per_device(): pl.pallas_call(functools.partial(kernel, n_pipe, n_seq, n_mp), out_shape=...  214 us

profile of v4, /device:TPU:0, one launch (start us, length us, event | category | flops | bytes accessed | tf_op | source)
XLA Modules:
  0.0 218.7 jit_solution(17133868796775106262)
XLA Ops:
  1.3 213.9 %shard_map.113 = (bf16[1,2,64,1024]{3,2,1,0:T(8,128)(2,1)}, bf16[1,2,2,64,1024]{4,3,2,1,0:T(8,128)(2,1)}) custom-call(bf16[2,64,4096]{2,1,0:T(8,128)(2,1)} %enc_ref.1, bf16[2,64,4096]{2,1,0:T(8,128)(2,1)} %dec_ref.1, s32[2,128]{1,0:T(2,128)} %doc_ref.1, s32[1]{0:T(128)S(6)} %copy.14.count_ref, f32[1,4096]{1,0:T(1,128)} %gain_ref.1, ...), custom_call_target="tpu_custom_call" | custom-call | tf_op jit(solution)/shard_map/pallas_call | solution.py:830
  215.2 1.7 copy.15
  216.9 1.9 copy.16

commit v5 on v4

--- a/solution.py
+++ b/solution.py
@@ -10,6 +10,7 @@
 HEADS = 8
 HS = 256
 PAD = 128
+SPLIT = 2
 
 epsilon = 1e-06
 MESH = pl.DeviceIdType.MESH
@@ -113,12 +114,14 @@
     pass_ssem,
     gb_ssem,
     gb_rsem,
+    clear_sem,
 ):
     pipe = lax.axis_index("pipe")
     seq = lax.axis_index("seq")
     z = lax.axis_index("mp")
     batches, toks, width = enc_ref.shape
     share = width // n_mp
+    part = share // SPLIT
     heads = HEADS // n_mp
     units = heads * HS
     scale = HS ** (-0.5)
@@ -179,17 +182,28 @@
     encoder = pipe < count_ref[0]
     prev_encoder = pipe - 1 < count_ref[0]
 
-    def cut(ref, m, j):
-        return ref[m, :, pl.ds(pl.multiple_of(j * share, share), share)]
-
-    def gain_of(j):
-        return gain_ref[:, pl.ds(pl.multiple_of(j * share, share), share)]
-
-    def chunk_rows(ref, j):
-        return ref[pl.ds(pl.multiple_of(j * share, share), share), :]
-
-    def chunk_cols(ref, j):
-        return ref[:, pl.ds(pl.multiple_of(j * share, share), share)]
+    def span(f, j):
+        return pl.ds(pl.multiple_of(j * share + f * part, part), part)
+
+    def cut(ref, m, f, j):
+        return ref[m, :, span(f, j)]
+
+    def gain_of(f, j):
+        return gain_ref[:, span(f, j)]
+
+    def chunk_rows(ref, f, j):
+        return ref[span(f, j), :]
+
+    def chunk_cols(ref, f, j):
+        return ref[:, span(f, j)]
+
+    def slabs(m):
+        return pl.ds(m * SPLIT, SPLIT)
+
+    pieces = SPLIT * n_mp
+
+    def piece(i):
+        return lax.div(i, n_mp), lax.rem(i, n_mp)
 
     length = n_seq * toks
     for m in range(batches):
@@ -210,7 +224,7 @@
         return kv_all[m, :, :, units + h * HS : units + (h + 1) * HS].reshape(length, HS)
 
     def enc_copy(m, device):
-        return copy(enc_cur.at[m], enc_recv.at[m], enc_ssem.at[m], enc_rsem.at[m], device)
+        return copy(enc_cur.at[slabs(m)], enc_recv.at[slabs(m)], enc_ssem.at[m], enc_rsem.at[m], device)
 
     def kv_copy(m, slot, peer, owner):
         return copy(
@@ -257,7 +271,9 @@
         )
 
     def gb_copy(m, device):
-        return copy(bhop.at[m], gb_recv.at[m], gb_ssem.at[m], gb_rsem.at[m], device)
+        return copy(
+            bhop.at[slabs(m)], gb_recv.at[slabs(m)], gb_ssem.at[m], gb_rsem.at[m], device
+        )
 
     chain = n_mp == 4
     far = n_mp - 1 - z
@@ -346,20 +362,21 @@
 
     @pl.when(is_end)
     def _():
-        for m in range(batches):
+        for p in range(batches * SPLIT):
             for recv in (fs_recv, a_recv, b_recv):
-                recv[m, far] = jnp.zeros((toks, share), BF16)
+                recv[p, far] = jnp.zeros((toks, part), BF16)
 
     hop_order = [lax.rem(z + k, n_mp) for k in sorted(range(n_mp), key=lambda k: (k == 0, k != 2))]
 
     def forward_a(m, wait_q):
         @pl.when(pipe == 0)
         def _():
-            def fill(j, carry):
-                upd_recv[m, j] = cut(enc_ref, m, j)
+            def fill(i, carry):
+                f, j = piece(i)
+                upd_recv[m * SPLIT + f, j] = cut(enc_ref, m, f, j)
                 return carry
 
-            lax.fori_loop(0, n_mp, fill, 0)
+            lax.fori_loop(0, pieces, fill, 0)
 
         @pl.when(pipe > 1)
         def _():
@@ -369,32 +386,34 @@
         v_acc[m] = jnp.zeros((toks, units), F32)
         q_acc[m] = jnp.zeros((toks, units), F32)
 
-        def project(k, sums):
+        def project(i, sums):
+            f, k = piece(i)
             j = gather_order(k)
+            p = m * SPLIT + f
 
             @pl.when(pipe > 0)
             def _():
-                upd_copy(m, j, j, at_mp(z)).wait_recv()
+                upd_copy(p, j, j, at_mp(z)).wait_recv()
 
                 @pl.when(jnp.logical_and(is_mid, k == 1))
                 def _():
-                    pass_copy(0, m, upd_recv, upd_rsem).start()
-
-            fresh = upd_recv[m, j].astype(F32)
-            enc = jnp.where(prev_encoder, fresh, enc_recv[m, j].astype(F32))
-            dec = jnp.where(prev_encoder, cut(dec_ref, m, j).astype(F32), fresh)
+                    pass_copy(0, p, upd_recv, upd_rsem).start()
+
+            fresh = upd_recv[p, j].astype(F32)
+            enc = jnp.where(prev_encoder, fresh, enc_recv[p, j].astype(F32))
+            dec = jnp.where(prev_encoder, cut(dec_ref, m, f, j).astype(F32), fresh)
             src = jnp.where(encoder, enc, dec)
-            enc_cur[m, j] = enc.astype(BF16)
-            src_cur[m, j] = src.astype(BF16)
-            m_part = (enc * gain_of(j)).astype(BF16)
-            k_acc[m] += dot_nn(m_part, chunk_rows(wk, j))
-            v_acc[m] += dot_nn(m_part, chunk_rows(wv, j))
+            enc_cur[p, j] = enc.astype(BF16)
+            src_cur[p, j] = src.astype(BF16)
+            m_part = (enc * gain_of(f, j)).astype(BF16)
+            k_acc[m] += dot_nn(m_part, chunk_rows(wk, f, j))
+            v_acc[m] += dot_nn(m_part, chunk_rows(wv, f, j))
             return (
                 sums[0] + jnp.sum(src * src, axis=-1, keepdims=True),
                 sums[1] + jnp.sum(enc * enc, axis=-1, keepdims=True),
             )
 
-        q_square, m_square = lax.fori_loop(0, n_mp, project, (none, none))
+        q_square, m_square = lax.fori_loop(0, pieces, project, (none, none))
         q_factor[m] = lax.rsqrt(q_square / width + epsilon)
         m_factor[m] = lax.rsqrt(m_square / width + epsilon)
 
@@ -415,12 +434,13 @@
         if wait_q:
             weight_loads[2].wait()
 
-        def project_q(j, carry):
-            q_part = (src_cur[m, j].astype(F32) * gain_of(j)).astype(BF16)
-            q_acc[m] += dot_nn(q_part, chunk_rows(wq, j))
+        def project_q(i, carry):
+            f, j = piece(i)
+            q_part = (src_cur[m * SPLIT + f, j].astype(F32) * gain_of(f, j)).astype(BF16)
+            q_acc[m] += dot_nn(q_part, chunk_rows(wq, f, j))
             return carry
 
-        lax.fori_loop(0, n_mp, project_q, 0)
+        lax.fori_loop(0, pieces, project_q, 0)
         for h in range(heads):
             lanes = slice(h * HS, (h + 1) * HS)
             found = q_acc[m, :, lanes] * q_factor[m]
@@ -443,28 +463,31 @@
             portion[m, h] = weights / totals
 
     def forward_out(m):
-        def emit(k, carry):
+        def emit(i, carry):
+            f, k = piece(i)
             j = reduce_order(k)
-            block = dot_nn(attended[m], chunk_cols(wo, j))
-            reduce_part(0, m, k, j, block, fs_send, fs_relay, fs_copy)
+            block = dot_nn(attended[m], chunk_cols(wo, f, j))
+            reduce_part(0, m * SPLIT + f, k, j, block, fs_send, fs_relay, fs_copy)
             return carry
 
-        lax.fori_loop(0, n_mp, emit, 0)
+        lax.fori_loop(0, pieces, emit, 0)
 
     def forward_c(m):
-        branch = reduced(m, fs_send, fs_recv, fs_copy)
-        updated = (src_cur[m, z].astype(F32) + branch).astype(BF16)
-        upd_send[m] = updated
-
-        @pl.when(pipe < last)
-        def _():
-            for j in hop_order:
-
-                @pl.when(kept(j))
-                def _():
-                    upd_copy(m, j, z, (pipe + 1, seq, j)).start()
-
-        so_ref[0, m] = updated
+        for f in range(SPLIT):
+            p = m * SPLIT + f
+            branch = reduced(p, fs_send, fs_recv, fs_copy)
+            updated = (src_cur[p, z].astype(F32) + branch).astype(BF16)
+            upd_send[p] = updated
+
+            @pl.when(pipe < last)
+            def _():
+                for j in hop_order:
+
+                    @pl.when(kept(j))
+                    def _():
+                        upd_copy(p, j, z, (pipe + 1, seq, j)).start()
+
+            so_ref[0, m, :, f * part : (f + 1) * part] = updated
 
     def sort_a(dq, dm):
         return jnp.where(encoder, dq + dm, jnp.where(prev_encoder, dm, dq))
@@ -484,29 +507,34 @@
     def backward_pull(m):
         @pl.when(pipe == last)
         def _():
-            def fill(j, carry):
-                start = cut(og_ref, m, j).astype(F32)
-                u_recv[m, j] = jnp.where(encoder, 0.0, start).astype(BF16)
+            def fill(i, carry):
+                f, j = piece(i)
+                start = cut(og_ref, m, f, j).astype(F32)
+                u_recv[m * SPLIT + f, j] = jnp.where(encoder, 0.0, start).astype(BF16)
                 return carry
 
-            lax.fori_loop(0, n_mp, fill, 0)
-            start = cut(og_ref, m, z).astype(F32)
-            gb_recv[m] = jnp.where(encoder, start, 0.0).astype(BF16)
-
-        def pull(k, total):
+            lax.fori_loop(0, pieces, fill, 0)
+            for f in range(SPLIT):
+                start = cut(og_ref, m, f, z).astype(F32)
+                gb_recv[m * SPLIT + f] = jnp.where(encoder, start, 0.0).astype(BF16)
+
+        def pull(i, total):
+            f, k = piece(i)
             j = gather_order(k)
+            p = m * SPLIT + f
 
             @pl.when(pipe < last)
             def _():
-                u_copy(m, j, j, at_mp(z)).wait_recv()
+                u_copy(p, j, j, at_mp(z)).wait_recv()
 
                 @pl.when(jnp.logical_and(is_mid, k == 1))
                 def _():
-                    pass_copy(1, m, u_recv, u_rsem).start()
-
-            return total + dot_nt(u_recv[m, j], chunk_cols(wo, j))
-
-        d_att[m] = lax.fori_loop(0, n_mp, pull, jnp.zeros((toks, units), F32)).astype(BF16)
+                    pass_copy(1, p, u_recv, u_rsem).start()
+
+            return total + dot_nt(u_recv[p, j], chunk_cols(wo, f, j))
+
+        d_att[m] = lax.fori_loop(
+            0, pieces, pull, jnp.zeros((toks, units), F32)).astype(BF16)
 
     def backward_a(m):
         for h in range(heads):
@@ -532,11 +560,12 @@
         for k in range(1, n_seq):
             kvg_copy(m, k, lax.rem(seq + k, n_seq), seq).start()
 
-        def ask(j, carry):
-            dq_buf[m, j] = dot_nt(q_grad[m], chunk_rows(wq, j))
+        def ask(i, carry):
+            f, j = piece(i)
+            dq_buf[m * SPLIT + f, j] = dot_nt(q_grad[m], chunk_rows(wq, f, j))
             return carry
 
-        lax.fori_loop(0, n_mp, ask, 0)
+        lax.fori_loop(0, pieces, ask, 0)
 
     def backward_b(m):
         q_stat = jnp.sum(q_grad[m].astype(F32) * q_acc[m], axis=-1, keepdims=True)
@@ -563,18 +592,20 @@
         for k in range(1, n_mp):
             stat_copy(m, lax.rem(z + k, n_mp), z).start()
 
-        def spread_out(k, carry):
+        def spread_out(i, carry):
+            f, k = piece(i)
+            p = m * SPLIT + f
             j = reduce_order(k)
-            dm = dot_nt(k_grad[m], chunk_rows(wk, j)) + dot_nt(v_grad[m], chunk_rows(wv, j))
-            dq = dq_buf[m, j]
-            reduce_part(1, m, k, j, sort_a(dq, dm), a_send, a_relay, a_copy)
-            b_send[m, j] = sort_b(dq, dm).astype(BF16)
+            dm = dot_nt(k_grad[m], chunk_rows(wk, f, j)) + dot_nt(v_grad[m], chunk_rows(wv, f, j))
+            dq = dq_buf[p, j]
+            reduce_part(1, p, k, j, sort_a(dq, dm), a_send, a_relay, a_copy)
+            b_send[p, j] = sort_b(dq, dm).astype(BF16)
             return carry
 
-        lax.fori_loop(0, n_mp, spread_out, 0)
-
-    def norm_back(values, factor, total, stat):
-        return factor * (gain_of(z) * total - values * (factor * factor * (stat / width)))
+        lax.fori_loop(0, pieces, spread_out, 0)
+
+    def norm_back(f, values, factor, total, stat):
+        return factor * (gain_of(f, z) * total - values * (factor * factor * (stat / width)))
 
     def backward_c(m):
         stats = s_send[m]
@@ -583,51 +614,60 @@
             stat_copy(m, j, j).wait_recv()
             stats = stats + s_recv[m, j]
         s_total[m] = stats
-        total = reduced(m, a_send, a_recv, a_copy)
-
-        @pl.when(pipe < last)
-        def _():
-            gb_copy(m, at_mp(z)).wait_recv()
-
-        base = jnp.where(turns, gb_recv[m].astype(F32), u_recv[m, z].astype(F32))
-        values = jnp.where(turns, enc_cur[m, z].astype(F32), src_cur[m, z].astype(F32))
         factor = jnp.where(turns, m_factor[m], q_factor[m])
-        fresh = base + norm_back(values, factor, total, to_column(stats[0:1, :]))
-        ahop[m] = fresh.astype(BF16)
-
-        @pl.when(pipe > 0)
-        def _():
-            for j in hop_order:
-
-                @pl.when(kept(j))
+        stat = to_column(stats[0:1, :])
+        for f in range(SPLIT):
+            p = m * SPLIT + f
+            total = reduced(p, a_send, a_recv, a_copy)
+            if f == 0:
+
+                @pl.when(pipe < last)
                 def _():
-                    u_copy(m, j, z, (pipe - 1, seq, j)).start()
-
-    def finish(m, b_new):
-        a_new = ahop[m].astype(F32)
-        sg_ref[0, 0, m] = jnp.where(first, a_new, b_new).astype(BF16)
-        sg_ref[0, 1, m] = jnp.where(first, b_new, a_new).astype(BF16)
+                    gb_copy(m, at_mp(z)).wait_recv()
+
+            base = jnp.where(turns, gb_recv[p].astype(F32), u_recv[p, z].astype(F32))
+            values = jnp.where(turns, enc_cur[p, z].astype(F32), src_cur[p, z].astype(F32))
+            fresh = base + norm_back(f, values, factor, total, stat)
+            ahop[p] = fresh.astype(BF16)
+
+            @pl.when(pipe > 0)
+            def _():
+                for j in hop_order:
+
+                    @pl.when(kept(j))
+                    def _():
+                        u_copy(p, j, z, (pipe - 1, seq, j)).start()
+
+    def finish(m, f, b_new):
+        a_new = ahop[m * SPLIT + f].astype(F32)
+        lanes = slice(f * part, (f + 1) * part)
+        sg_ref[0, 0, m, :, lanes] = jnp.where(first, a_new, b_new).astype(BF16)
+        sg_ref[0, 1, m, :, lanes] = jnp.where(first, b_new, a_new).astype(BF16)
 
     def backward_d(m):
         @pl.when(pipe == 0)
         def _():
-            finish(m, gb_recv[m].astype(F32))
+            for f in range(SPLIT):
+                finish(m, f, gb_recv[m * SPLIT + f].astype(F32))
 
         @pl.when(pipe > 0)
         def _():
-            total = reduced(m, b_send, b_recv, b_copy)
-            base = jnp.where(turns, u_recv[m, z].astype(F32), gb_recv[m].astype(F32))
-            values = jnp.where(turns, src_cur[m, z].astype(F32), enc_cur[m, z].astype(F32))
             factor = jnp.where(turns, q_factor[m], m_factor[m])
-            fresh = base + norm_back(values, factor, total, to_column(s_total[m, 1:2, :]))
-            bhop[m] = fresh.astype(BF16)
+            stat = to_column(s_total[m, 1:2, :])
+            for f in range(SPLIT):
+                p = m * SPLIT + f
+                total = reduced(p, b_send, b_recv, b_copy)
+                base = jnp.where(turns, u_recv[p, z].astype(F32), gb_recv[p].astype(F32))
+                values = jnp.where(turns, src_cur[p, z].astype(F32), enc_cur[p, z].astype(F32))
+                fresh = base + norm_back(f, values, factor, total, stat)
+                bhop[p] = fresh.astype(BF16)
+                finish(m, f, fresh)
             gb_copy(m, (pipe - 1, seq, z)).start()
-            finish(m, fresh)
 
     def backward_rest():
         @pl.when(pipe > 0)
         def _():
-            for m in range(batches):
+            for m in range(batches * SPLIT):
                 for j in hop_order:
 
                     @pl.when(kept(j))
@@ -648,7 +688,7 @@
 
             @pl.when(is_mid)
             def _():
-                for m in range(batches):
+                for m in range(batches * SPLIT):
                     relay_copy(2, m, b_send, b_relay).wait_recv()
                     joined = b_send[m, other_end].astype(F32) + b_relay[m].astype(F32)
                     b_send[m, other_end] = joined.astype(BF16)
@@ -682,6 +722,12 @@
         backward_c(batches - 1)
         backward_rest()
 
+        @pl.when(pipe == last - 1)
+        def _():
+            pl.semaphore_signal(
+                clear_sem, inc=1, device_id=(pipe + 1, seq, z), device_id_type=MESH
+            )
+
     @pl.when(pipe == last)
     def _():
         for load in weight_loads:
@@ -700,6 +746,8 @@
             backward_b(m)
         backward_c(batches - 1)
         backward_rest()
+        if last > 0:
+            pl.semaphore_wait(clear_sem, 1)
         for m in range(batches):
             forward_out(m)
         for m in range(batches):
@@ -716,39 +764,41 @@
             kv_copy(m, k, peer, seq).wait_send()
             kvg_copy(m, k, peer, seq).wait_send()
         for k in range(1, n_mp):
-            j = lax.rem(z + k, n_mp)
-            stat_copy(m, j, z).wait_send()
-        reduce_drain(0, m, fs_send, fs_relay, fs_copy)
-        reduce_drain(1, m, a_send, a_relay, a_copy)
+            stat_copy(m, lax.rem(z + k, n_mp), z).wait_send()
+    for p in range(batches * SPLIT):
+        reduce_drain(0, p, fs_send, fs_relay, fs_copy)
+        reduce_drain(1, p, a_send, a_relay, a_copy)
 
     @pl.when(pipe < last)
     def _():
-        for m in range(batches):
+        for p in range(batches * SPLIT):
             for j in hop_order:
 
                 @pl.when(kept(j))
                 def _():
-                    upd_copy(m, j, z, (pipe + 1, seq, j)).wait_send()
+                    upd_copy(p, j, z, (pipe + 1, seq, j)).wait_send()
 
             @pl.when(is_mid)
             def _():
-                pass_copy(1, m, u_recv, u_rsem).wait_send()
+                pass_copy(1, p, u_recv, u_rsem).wait_send()
 
     @pl.when(pipe > 0)
     def _():
         for m in range(batches):
             gb_copy(m, (pipe - 1, seq, z)).wait_send()
-            reduce_drain(2, m, b_send, b_relay, b_copy)
+        for p in range(batches * SPLIT):
+            reduce_drain(2, p, b_send, b_relay, b_copy)
 
             @pl.when(is_mid)
             def _():
-                pass_copy(0, m, upd_recv, upd_rsem).wait_send()
+                pass_copy(0, p, upd_recv, upd_rsem).wait_send()
 
 
 def per_device(n_pipe, n_seq, n_mp, enc_in, dec_in, doc_ids, enc_sections, norm_gain,
                q_weight, k_weight, v_weight, o_weight, out_grad):
     batches, toks, width = enc_in.shape
     share = width // n_mp
+    part = share // SPLIT
     heads = HEADS // n_mp
     units = heads * HS
     length = n_seq * toks
@@ -764,10 +814,10 @@
         V((units, width), BF16),
         dma((4,)),
         V((batches, length, length), F32),
-        V((batches, n_mp, toks, share), BF16),
-        V((batches, n_mp, toks, share), BF16),
-        V((batches, n_mp, toks, share), BF16),
-        V((batches, n_mp, toks, share), BF16),
+        V((batches * SPLIT, n_mp, toks, part), BF16),
+        V((batches * SPLIT, n_mp, toks, part), BF16),
+        V((batches * SPLIT, n_mp, toks, part), BF16),
+        V((batches * SPLIT, n_mp, toks, part), BF16),
         V((batches, toks, units), F32),
         V((batches, toks, units), F32),
         V((batches, toks, units), F32),
@@ -779,53 +829,54 @@
         V((batches, n_seq, toks, 2 * units), BF16),
         V((batches, heads, toks, length), F32),
         V((batches, toks, units), BF16),
-        V((batches, n_mp, toks, share), BF16),
-        V((batches, n_mp, toks, share), BF16),
-        V((batches, toks, share), BF16),
-        V((batches, n_mp, toks, share), BF16),
+        V((batches * SPLIT, n_mp, toks, part), BF16),
+        V((batches * SPLIT, n_mp, toks, part), BF16),
+        V((batches * SPLIT, toks, part), BF16),
+        V((batches * SPLIT, n_mp, toks, part), BF16),
         V((batches, toks, units), BF16),
         V((batches, n_seq, toks, 2 * units), BF16),
         V((batches, n_seq, toks, 2 * units), BF16),
         V((batches, toks, units), BF16),
         V((batches, toks, units), BF16),
         V((batches, toks, units), BF16),
-        V((batches, n_mp, toks, share), F32),
-        V((batches, n_mp, toks, share), BF16),
-        V((batches, n_mp, toks, share), BF16),
-        V((batches, n_mp, toks, share), BF16),
-        V((batches, n_mp, toks, share), BF16),
+        V((batches * SPLIT, n_mp, toks, part), F32),
+        V((batches * SPLIT, n_mp, toks, part), BF16),
+        V((batches * SPLIT, n_mp, toks, part), BF16),
+        V((batches * SPLIT, n_mp, toks, part), BF16),
+        V((batches * SPLIT, n_mp, toks, part), BF16),
         V((batches, 8, PAD), F32),
         V((batches, n_mp, 8, PAD), F32),
         V((batches, 8, PAD), F32),
-        V((batches, toks, share), BF16),
-        V((batches, toks, share), BF16),
-        V((batches, toks, share), BF16),
-        V((batches, toks, share), BF16),
-        V((batches, toks, share), BF16),
-        V((batches, toks, share), BF16),
-        dma((batches, n_mp)),
-        dma((batches, n_mp)),
+        V((batches * SPLIT, toks, part), BF16),
+        V((batches * SPLIT, toks, part), BF16),
+        V((batches * SPLIT, toks, part), BF16),
+        V((batches * SPLIT, toks, part), BF16),
+        V((batches * SPLIT, toks, part), BF16),
+        V((batches * SPLIT, toks, part), BF16),
+        dma((batches * SPLIT, n_mp)),
+        dma((batches * SPLIT, n_mp)),
         dma((batches,)),
         dma((batches,)),
         dma((batches, n_seq)),
         dma((batches, n_seq)),
+        dma((batches * SPLIT, n_mp)),
+        dma((batches * SPLIT, n_mp)),
+        dma((batches * SPLIT, n_mp)),
+        dma((batches * SPLIT, n_mp)),
+        dma((batches, n_seq)),
+        dma((batches, n_seq)),
+        dma((batches * SPLIT, n_mp)),
+        dma((batches * SPLIT, n_mp)),
+        dma((batches * SPLIT, n_mp)),
+        dma((batches * SPLIT, n_mp)),
         dma((batches, n_mp)),
         dma((batches, n_mp)),
-        dma((batches, n_mp)),
-        dma((batches, n_mp)),
-        dma((batches, n_seq)),
-        dma((batches, n_seq)),
-        dma((batches, n_mp)),
-        dma((batches, n_mp)),
-        dma((batches, n_mp)),
-        dma((batches, n_mp)),
-        dma((batches, n_mp)),
-        dma((batches, n_mp)),
-        dma((3, batches)),
-        dma((3, batches)),
-        dma((2, batches)),
+        dma((3, batches * SPLIT)),
+        dma((3, batches * SPLIT)),
+        dma((2, batches * SPLIT)),
         dma((batches,)),
         dma((batches,)),
+        pltpu.SemaphoreType.REGULAR,
     ]
     return pl.pallas_call(
         functools.partial(kernel, n_pipe, n_seq, n_mp),

time: 219 us -> 219 us (level)
  no operation moved by 1% of the time
where the time goes in v5:
time: 219 us
  Pallas kernels  214 us (98%)
  local copies, waits for them, and re-layouts  3.54 us (2%)
    pallas_call x1, Pallas kernels, per_device(): pl.pallas_call(functools.partial(kernel, n_pipe, n_seq, n_mp), out_shape=...  214 us

profile of v5, /device:TPU:0, one launch (start us, length us, event | category | flops | bytes accessed | tf_op | source)
XLA Modules:
  0.0 219.2 jit_solution(9689891204504023484)
XLA Ops:
  1.3 214.4 %shard_map.113 = (bf16[1,2,64,1024]{3,2,1,0:T(8,128)(2,1)}, bf16[1,2,2,64,1024]{4,3,2,1,0:T(8,128)(2,1)}) custom-call(bf16[2,64,4096]{2,1,0:T(8,128)(2,1)} %enc_ref.1, bf16[2,64,4096]{2,1,0:T(8,128)(2,1)} %dec_ref.1, s32[2,128]{1,0:T(2,128)} %doc_ref.1, s32[1]{0:T(128)S(6)} %copy.14.count_ref, f32[1,4096]{1,0:T(1,128)} %gain_ref.1, ...), custom_call_target="tpu_custom_call" | custom-call | tf_op jit(solution)/shard_map/pallas_call | solution.py:881
  215.7 1.7 copy.15
  217.3 1.9 copy.16

commit v6 on v5

--- a/solution.py
+++ b/solution.py
@@ -149,7 +149,7 @@
             [(wk_hbm, wk), (wv_hbm, wv), (wq_hbm, wq), (wo_hbm, wo)]
         )
     ]
-    for load in weight_loads:
+    for load in weight_loads[:2]:
         load.start()
 
     barrier = pltpu.get_barrier_semaphore()
@@ -178,6 +178,9 @@
 
     edge = jnp.where(pipe > 0, n_mp, 0) + jnp.where(pipe < last, n_mp, 0)
     pl.semaphore_wait(barrier, n_mp - 1 + n_seq - 1 + edge)
+
+    for load in weight_loads[2:]:
+        load.start()
 
     encoder = pipe < count_ref[0]
     prev_encoder = pipe - 1 < count_ref[0]
@@ -621,11 +624,18 @@
             total = reduced(p, a_send, a_recv, a_copy)
             if f == 0:
 
-                @pl.when(pipe < last)
+                @pl.when(jnp.logical_and(pipe > 0, pipe < last))
                 def _():
                     gb_copy(m, at_mp(z)).wait_recv()
 
-            base = jnp.where(turns, gb_recv[p].astype(F32), u_recv[p, z].astype(F32))
+            own = u_recv[p, z].astype(F32)
+            ahop[p] = own.astype(BF16)
+
+            @pl.when(pipe > 0)
+            def _():
+                ahop[p] = jnp.where(turns, gb_recv[p].astype(F32), own).astype(BF16)
+
+            base = ahop[p].astype(F32)
             values = jnp.where(turns, enc_cur[p, z].astype(F32), src_cur[p, z].astype(F32))
             fresh = base + norm_back(f, values, factor, total, stat)
             ahop[p] = fresh.astype(BF16)
@@ -647,6 +657,8 @@
     def backward_d(m):
         @pl.when(pipe == 0)
         def _():
+            if last > 0:
+                gb_copy(m, at_mp(z)).wait_recv()
             for f in range(SPLIT):
                 finish(m, f, gb_recv[m * SPLIT + f].astype(F32))
 

time: 219 us -> 219 us (level)
  no operation moved by 1% of the time
where the time goes in v6:
time: 219 us
  Pallas kernels  214 us (98%)
  local copies, waits for them, and re-layouts  3.54 us (2%)
    pallas_call x1, Pallas kernels, per_device(): pl.pallas_call(functools.partial(kernel, n_pipe, n_seq, n_mp), out_shape=...  214 us

profile of v6, /device:TPU:0, one launch (start us, length us, event | category | flops | bytes accessed | tf_op | source)
XLA Modules:
  0.0 219.2 jit_solution(17717825772604587049)
XLA Ops:
  1.3 214.4 %shard_map.113 = (bf16[1,2,64,1024]{3,2,1,0:T(8,128)(2,1)}, bf16[1,2,2,64,1024]{4,3,2,1,0:T(8,128)(2,1)}) custom-call(bf16[2,64,4096]{2,1,0:T(8,128)(2,1)} %enc_ref.1, bf16[2,64,4096]{2,1,0:T(8,128)(2,1)} %dec_ref.1, s32[2,128]{1,0:T(2,128)} %doc_ref.1, s32[1]{0:T(128)S(6)} %copy.14.count_ref, f32[1,4096]{1,0:T(1,128)} %gain_ref.1, ...), custom_call_target="tpu_custom_call" | custom-call | tf_op jit(solution)/shard_map/pallas_call | solution.py:893
  215.6 1.7 copy.15
  217.3 1.9 copy.16
